TPU v7x, 256 devices: a whole 4x4x8 slice. The times are simulated.
256 devices in a mesh: fsdp: 16 (over y, z_lo), expert: 16 (over z_hi, x, core).
Axes of the slice: x: 4, y: 4, z: 8 (z_hi: 2, z_lo: 4; z = z_hi * 4 + z_lo), core: 2. Of those that a mesh axis runs over, the one named last changes fastest.
Arguments:
- tokens: bfloat16 [16, 2048, 2048], P('fsdp', 'expert'), may hold values from -6 to 6
- doc_ids: int32 [16, 2048], P('fsdp'), may hold values from 0 to 7, never falling along the last dimension, each value on 1 to 512 neighbouring positions
- route_ids: int32 [16, 2048, 10], P('fsdp', 'expert'), may hold values from 0 to 15, all different within a row; in each aligned block of 128 rows (0 to 127, 128 to 255, ..., all dimensions but the last counted through in order) at most 88 rows name the same one
- norm_gain: bfloat16 [2048], replicated, may hold values from 0.25 to 1.75
- proj_weight: bfloat16 [2048, 16, 512], P('fsdp', 'expert'), may hold values from -0.125 to 0.125
- gating_weight: bfloat16 [2048, 2, 16], P('fsdp', None, 'expert'), may hold values from -0.125 to 0.125
- block_scale: bfloat16 [16, 16, 4], P('fsdp', 'expert'), may hold values from 0.5 to 2
- conv_weight: bfloat16 [16, 4, 384], P('expert'), may hold values from -3 to 3
- decay_rate: float32 [16], P('expert'), may hold values from 0.005 to 0.1
- head_gain: bfloat16 [128], replicated, may hold values from 0.25 to 1.75
- out_weight: bfloat16 [16, 128, 2048], P('expert', None, 'fsdp'), may hold values from -0.125 to 0.125
- moe_gain: bfloat16 [2048], replicated, may hold values from 0.25 to 1.75
- router_weight: bfloat16 [2048, 16], replicated, may hold values from -0.125 to 0.125
- expert_in: bfloat16 [16, 2048, 1024], P('expert'), may hold values from -0.125 to 0.125
- expert_out: bfloat16 [16, 512, 2048], P('expert'), may hold values from -0.25 to 0.25
Outputs:
- mixed_out: bfloat16 [16, 2048, 2048], P('fsdp', 'expert')
Inputs may be any that keep to these rules, and one draw needn't show every extreme that they name: `route_ids`: each token names 10 different experts. Among the 128 tokens of one device (aligned blocks of 128 token rows in order) no expert is named by more than 88 tokens, and in every draw some expert is named by exactly 88. `doc_ids`: along each sequence the ids never fall; a document spans 1 to 512 positions and one spans exactly 512.
All inputs are finite; a program needn't handle non-finite values.
Results may differ from a plain program's by a relative error of at most 0.015.
Values may be sent and summed in bfloat16 or wider, within the bound.
A program may use at most 128 MiB of HBM per device.

v0:
```python
import jax
import jax.numpy as jnp
from jax import lax
from jax.sharding import PartitionSpec as P

D = 2048
FF = 512
HD = 128
QB = 128
BLOCK = 128
EXPERTS = 16
TOP = 10
CAP = 88


def rms_scale(values, gain):
    mean_square = jnp.mean(values * values, axis=-1, keepdims=True)
    return values * lax.rsqrt(mean_square + 1e-06) * gain.astype(jnp.float32)


def short_conv(channels, conv_weight, seq_docs):
    tap_count = conv_weight.shape[1]
    summed = channels * conv_weight[:, 0, :].astype(jnp.float32)
    for shift_by in range(1, tap_count):
        moved = jnp.concatenate(
            [jnp.zeros((shift_by,) + channels.shape[1:], jnp.float32), channels[:-shift_by]], 0
        )
        moved_docs = jnp.concatenate(
            [jnp.full((shift_by,), -1, jnp.int32), seq_docs[:-shift_by]], 0
        )
        keep_mask = (moved_docs == seq_docs).astype(jnp.float32)[:, None, None]
        summed = summed + moved * keep_mask * conv_weight[:, shift_by, :].astype(jnp.float32)
    return jax.nn.silu(summed)


def prepare(projected, gate_inputs, seq_docs, conv_weight, decay_rate):
    seq_len, head_count = (projected.shape[0], projected.shape[1])
    widened = projected.astype(jnp.float32)
    mixed_in = widened[:, :, 0:3, :].reshape(seq_len, head_count, 3 * HD)
    activated = short_conv(mixed_in, conv_weight, seq_docs)
    queries = activated[..., :HD]
    key_vecs = activated[..., HD : 2 * HD]
    value_vecs = activated[..., 2 * HD :]
    queries = (
        queries
        * lax.rsqrt(jnp.sum(queries * queries, axis=-1, keepdims=True) + 1e-06)
        * HD ** (-0.5)
    )
    key_vecs = key_vecs * lax.rsqrt(jnp.sum(key_vecs * key_vecs, axis=-1, keepdims=True) + 1e-06)
    beta_vals = jax.nn.sigmoid(gate_inputs[:, 0, :])
    log_gate = -decay_rate[None, :] * jax.nn.softplus(gate_inputs[:, 1, :])
    return (queries, key_vecs, value_vecs, beta_vals, log_gate, widened[:, :, 3, :])


def gated_output(recurrent, gate_branch, head_gain):
    return (rms_scale(recurrent, head_gain) * jax.nn.silu(gate_branch)).astype(jnp.bfloat16)


def block_rule(queries, key_vecs, value_vecs, beta_vals, log_gate, seq_docs):
    highest_precision = lax.Precision.HIGHEST
    seq_len, head_count, head_width = queries.shape
    num_blocks = seq_len // BLOCK

    def by_block(array):
        return jnp.swapaxes(array.reshape((num_blocks, BLOCK) + array.shape[1:]), 1, 2)

    query_blk = by_block(queries)
    key_blk = by_block(key_vecs)
    value_blk = by_block(value_vecs)
    beta_blk = by_block(beta_vals)
    cum_gate = jnp.cumsum(by_block(log_gate), axis=2)
    doc_blk = seq_docs.reshape(num_blocks, BLOCK)
    prev_doc = jnp.concatenate([jnp.full((1,), -1, jnp.int32), doc_blk[:-1, -1]], 0)
    start_gate = jnp.exp(cum_gate) * (doc_blk == prev_doc[:, None]).astype(jnp.float32)[:, None, :]
    position = jnp.arange(BLOCK)
    lower_mask = position[:, None] >= position[None, :]
    strict_mask = (position[:, None] > position[None, :]).astype(jnp.float32)
    same_doc = doc_blk[:, :, None] == doc_blk[:, None, :]
    keep_mask = (lower_mask[None] & same_doc)[:, None, :, :]
    log_gap = cum_gate[:, :, :, None] - cum_gate[:, :, None, :]
    decay_pair = jnp.where(keep_mask, jnp.exp(jnp.where(keep_mask, log_gap, 0.0)), 0.0)
    key_key = jnp.einsum("chld,chmd->chlm", key_blk, key_blk, precision=highest_precision)
    system = (
        jnp.eye(BLOCK, dtype=jnp.float32) + beta_blk[..., None] * key_key * decay_pair * strict_mask
    )
    right_side = jnp.concatenate(
        [beta_blk[..., None] * value_blk, (beta_blk * start_gate)[..., None] * key_blk], axis=-1
    )
    solved = jax.scipy.linalg.solve_triangular(system, right_side, lower=True, unit_diagonal=True)
    fresh_vals = solved[..., :head_width]
    carried = solved[..., head_width:]
    query_key = (
        jnp.einsum("chld,chmd->chlm", query_blk, key_blk, precision=highest_precision) * decay_pair
    )
    key_end = key_blk * decay_pair[:, :, -1, :, None]
    gate_end = start_gate[:, :, -1]

    def advance(recurrent_memory, inputs):
        fresh_in, carried_in, pair_in, query_inputs, key_inputs, gate_in, end_in = inputs
        new_vals = fresh_in - jnp.einsum(
            "hld,hde->hle", carried_in, recurrent_memory, precision=highest_precision
        )
        outputs = gate_in[..., None] * jnp.einsum(
            "hld,hde->hle", query_inputs, recurrent_memory, precision=highest_precision
        )
        outputs = outputs + jnp.einsum(
            "hlm,hme->hle", pair_in, new_vals, precision=highest_precision
        )
        recurrent_memory = end_in[:, None, None] * recurrent_memory + jnp.einsum(
            "hld,hle->hde", key_inputs, new_vals, precision=highest_precision
        )
        return (recurrent_memory, outputs)

    initial = jnp.zeros((head_count, head_width, head_width), jnp.float32)
    _, outputs = lax.scan(
        advance, initial, (fresh_vals, carried, query_key, query_blk, key_end, start_gate, gate_end)
    )
    return jnp.swapaxes(outputs, 1, 2).reshape(seq_len, head_count, head_width)


def head_products(head_rows_in, weights):
    products = jnp.einsum("thc,hcd->thd", head_rows_in, weights, preferred_element_type=jnp.float32)
    return lax.optimization_barrier(products.astype(jnp.bfloat16)).astype(jnp.float32)


def on_device(
    tokens,
    doc_ids,
    route_ids,
    norm_gain,
    proj_weight,
    gating_weight,
    block_scale,
    conv_weight,
    decay_rate,
    head_gain,
    out_weight,
    moe_gain,
    router_weight,
    expert_in,
    expert_out,
):
    own_rows = tokens[0]
    tok_count = own_rows.shape[0]
    residual = own_rows.astype(jnp.float32)
    normed_own = rms_scale(residual, norm_gain).astype(jnp.bfloat16)
    sequence = lax.all_gather(normed_own, "expert", axis=0, tiled=True)
    seq_docs = doc_ids[0]
    seq_len = sequence.shape[0]
    head_count = proj_weight.shape[1]
    block_count = proj_weight.shape[0] // QB
    main_blocks = proj_weight.reshape(block_count, QB, head_count, 4 * HD)
    gate_blocks = gating_weight.reshape(block_count, QB, 2, head_count)
    initial = (
        jnp.zeros((seq_len, head_count, 4, HD), jnp.float32),
        jnp.zeros((seq_len, 2, head_count), jnp.float32),
    )
    main_piece = lax.all_gather(main_blocks, "fsdp", axis=0, tiled=True)
    gate_piece = lax.all_gather(gate_blocks, "fsdp", axis=0, tiled=True)
    scale_piece = lax.all_gather(block_scale, "fsdp", axis=0, tiled=True)

    def one_block(block_idx, partial_sums):
        proj_sum, gate_sum = partial_sums
        columns = lax.dynamic_slice_in_dim(sequence, block_idx * QB, QB, 1)
        block_part = jnp.einsum(
            "tq,qhc->thc", columns, main_piece[block_idx], preferred_element_type=jnp.float32
        )
        block_part = (
            block_part.reshape(seq_len, head_count, 4, HD)
            * scale_piece[block_idx].astype(jnp.float32)[None, :, :, None]
        )
        gate_part = jnp.einsum(
            "tq,qgh->tgh", columns, gate_piece[block_idx], preferred_element_type=jnp.float32
        )
        return (proj_sum + block_part, gate_sum + gate_part)

    total_proj, gate_inputs = lax.fori_loop(0, main_piece.shape[0], one_block, initial)
    projected = total_proj.astype(jnp.bfloat16)
    queries, key_vecs, value_vecs, beta_vals, log_gate, gate_branch = prepare(
        projected, gate_inputs, seq_docs, conv_weight, decay_rate
    )
    recurrent = block_rule(queries, key_vecs, value_vecs, beta_vals, log_gate, seq_docs)
    head_out = gated_output(recurrent, gate_branch, head_gain)
    out_columns = lax.all_gather(out_weight, "fsdp", axis=2, tiled=True)
    attn_out = jnp.sum(
        lax.psum_scatter(
            head_products(head_out, out_columns).astype(jnp.bfloat16),
            "expert",
            scatter_dimension=0,
            tiled=True,
        ).astype(jnp.float32),
        axis=1,
    )
    mid_stream = residual + attn_out
    moe_in = rms_scale(mid_stream, moe_gain).astype(jnp.bfloat16)
    logits = jnp.dot(moe_in, router_weight, preferred_element_type=jnp.float32)
    route_own = route_ids[0]
    expert_range = jnp.arange(EXPERTS, dtype=jnp.int32)
    pick_mask = route_own[:, :, None] == expert_range[None, None, :]
    chosen = jnp.sum(jnp.where(pick_mask, logits[:, None, :], 0.0), axis=2)
    raised = jnp.exp(chosen)
    route_weight = raised / jnp.sum(raised, axis=1, keepdims=True)
    pick_flat = pick_mask.reshape(tok_count * TOP, EXPERTS).astype(jnp.int32)
    ranks = jnp.sum(jnp.cumsum(pick_flat, axis=0) * pick_flat, axis=1) - 1
    slot_ids = route_own.reshape(-1) * CAP + ranks
    owner_token = jnp.repeat(jnp.arange(tok_count, dtype=jnp.int32), TOP)
    row_table = jnp.full((EXPERTS * CAP,), tok_count, jnp.int32).at[slot_ids].set(owner_token)
    padded = jnp.concatenate([moe_in, jnp.zeros((1, D), jnp.bfloat16)], 0)
    owner_count = lax.axis_size("expert")
    outgoing = padded[row_table].reshape(owner_count, EXPERTS // owner_count, CAP, D)
    gate_up = jnp.einsum(
        "sjcd,jdf->sjcf",
        lax.all_to_all(outgoing, "expert", split_axis=0, concat_axis=0, tiled=True),
        expert_in,
        preferred_element_type=jnp.float32,
    )
    hidden = (jax.nn.silu(gate_up[..., :FF]) * gate_up[..., FF:]).astype(jnp.bfloat16)
    result = jnp.einsum(
        "sjcf,jfd->sjcd", hidden, expert_out, preferred_element_type=jnp.float32
    ).astype(jnp.bfloat16)
    returned_rows = lax.all_to_all(result, "expert", split_axis=0, concat_axis=0, tiled=True)
    gathered_out = returned_rows.reshape(EXPERTS * CAP, D)[slot_ids].reshape(tok_count, TOP, D)
    gathered_out = lax.optimization_barrier(gathered_out).astype(jnp.float32)
    moe_out = jnp.sum(route_weight[:, :, None] * gathered_out, axis=1)
    return (mid_stream + moe_out).astype(jnp.bfloat16)[None]


def solution(mesh):
    placed = (
        P("fsdp", "expert", None),
        P("fsdp", None),
        P("fsdp", "expert", None),
        P(),
        P("fsdp", "expert", None),
        P("fsdp", None, "expert"),
        P("fsdp", "expert", None),
        P("expert", None, None),
        P("expert"),
        P(),
        P("expert", None, "fsdp"),
        P(),
        P(),
        P("expert", None, None),
        P("expert", None, None),
    )
    return jax.shard_map(
        on_device, mesh=mesh, in_specs=placed, out_specs=P("fsdp", "expert", None), check_vma=False
    )
```

profile of v0, /device:TPU:79, one launch (start us, length us, event | category | flops | bytes accessed | tf_op | source)
XLA Modules:
  0.0 1114.7 jit_solution(2681577011354080930)
XLA Ops:
  9.2 2.0 fusion.67
  13.6 26.2 %all_gather.17 = bf16[16,1,4]{2,1,0:T(2,128)(2,1)S(1)} all-gather(bf16[1,1,4]{2,1,0:T(2,128)(2,1)} %param.25), channel_id=1, replica_groups=mesh['fsdp'=16,'expert'=16] {'fsdp'}, dimensions={0}, use_global_device_ids=true | all-gather | bytes 136 | tf_op jit(solution)/shard_map/all_gather | solution.py:160
  39.8 30.9 %all-gather.1 = bf16[2048,2,1]{0,1,2:T(2,128)(2,1)S(1)} all-gather(bf16[128,2,1]{0,1,2:T(2,128)(2,1)} %param.24), channel_id=3, replica_groups=mesh['fsdp'=16,'expert'=16] {'fsdp'}, dimensions={0}, use_global_device_ids=true | all-gather | bytes 8704 | tf_op jit(solution)/shard_map/all_gather | solution.py:159
  73.5 38.7 %all_gather.19 = bf16[1,128,2048]{2,1,0:T(8,128)(2,1)} all-gather(bf16[1,128,128]{2,1,0:T(8,128)(2,1)} %param.29), channel_id=1, replica_groups=mesh['fsdp'=16,'expert'=16] {'fsdp'}, dimensions={2}, use_global_device_ids=true | all-gather | bytes 557056 | tf_op jit(solution)/shard_map/all_gather | solution.py:184
  112.2 94.8 %all-gather.5.cloned.1.call-done = bf16[2048,2048]{1,0:T(8,128)(2,1)} async-done(((bf16[128,2048]{1,0:T(8,128)(2,1)}), bf16[2048,2048]{1,0:T(8,128)(2,1)}) %all-gather.5.cloned.1.call-update) | async-done | bytes 8388624 | tf_op jit(solution)/shard_map/all_gather | solution.py:147
  207.0 117.5 %while.29 = (s32[]{:T(128)}, f32[2048,1,4,128]{3,0,2,1:T(8,128)}, f32[2048,2,1]{0,1,2:T(2,128)S(1)}, bf16[2048,2048]{1,0:T(8,128)(2,1)}, bf16[16,128,1,512]{3,1,...) while((s32[]{:T(128)}, f32[2048,1,4,128]{3,0,2,1:T(8,128)}, ...), condition=%wide.region_2.0_spmd.clone, body=%wide.region_1.0_spmd.clone.sunk | while | flops 272637952 | bytes 10126558 | solution.py:177
  208.1 3.7 bitcast_add_fusion.2
  214.2 5.1 bitcast_add_fusion.2
  221.6 5.1 bitcast_add_fusion.2
  229.1 5.1 bitcast_add_fusion.2
  236.5 5.1 bitcast_add_fusion.2
  243.9 5.1 bitcast_add_fusion.2
  251.3 5.1 bitcast_add_fusion.2
  258.8 5.1 bitcast_add_fusion.2
  266.2 5.1 bitcast_add_fusion.2
  273.6 5.1 bitcast_add_fusion.2
  281.0 5.1 bitcast_add_fusion.2
  288.5 5.1 bitcast_add_fusion.2
  295.9 5.1 bitcast_add_fusion.2
  303.3 5.1 bitcast_add_fusion.2
  310.8 5.1 bitcast_add_fusion.2
  318.2 5.1 bitcast_add_fusion.2
  324.5 4.7 copy.69
  329.2 1.9 slice.142
  332.4 2.5 convert_element_type.233
  334.9 3.3 divide_multiply_fusion
  343.5 4.6 fusion.55
  348.1 5.3 fusion.61
  353.4 159.1 %custom-call.4 = f32[16,1,128,128]{2,3,1,0:T(8,128)} custom-call(f32[16,1,128,128]{3,2,1,0:T(8,128)} %fusion.61), custom_call_target="InvertDiagBlocksLowerTriangular" | custom-call | tf_op jit(solution)/shard_map/jit(_solve_triangular)/vmap()/triangular_solve | solution.py:89
  512.4 2.5 copy.73
  518.4 2.0 fusion.52
  522.3 89.6 %while.30 = (s32[]{:T(128)}, f32[1,128,128]{2,1,0:T(8,128)S(1)}, f32[16,1,128,128]{3,2,1,0:T(8,128)S(1)}, f32[16,1]{0,1:T(1,128)S(1)}, f32[16,1,128,128]{3,2,1,0...) while((s32[]{:T(128)}, f32[1,128,128]{2,1,0:T(8,128)S(1)}, ...), condition=%wide.region_7.8_spmd.clone, body=%wide.region_6.7_spmd.clone.sunk | while | flops 100794368 | bytes 988305 | solution.py:115
  526.1 1.8 fusion.134
  531.7 1.8 fusion.134
  537.3 1.8 fusion.134
  614.5 7.1 convert_bitcast_fusion
  622.7 4.5 reduce-window.6
  628.5 5.2 scatter_custom_fusion
  633.8 125.6 %reduce-scatter.2.cloned.1.call-done = bf16[128,1,2048]{2,0,1:T(8,128)(2,1)} async-done(((bf16[2048,1,2048]{2,0,1:T(8,128)(2,1)}), bf16[128,1,2048]{2,0,1:T(8,128)(2,1)}) %reduce-scatter.2.cloned.1.call-update) | async-done | bytes 524304 | tf_op jit(solution)/shard_map/reduce_scatter | solution.py:186
  762.7 6.9 gather_fusion
  769.6 139.8 %all_to_all.10 = bf16[16,1,88,2048]{3,2,1,0:T(8,128)(2,1)S(1)} all-to-all(bf16[16,1,88,2048]{3,2,1,0:T(8,128)(2,1)} %bitcast.260), channel_id=1, replica_groups=mesh['fsdp'=16,'expert'=16] {'expert'}, dimensions={0} | all-to-all | bytes 11534336 | tf_op jit(solution)/shard_map/all_to_all | solution.py:213
  909.5 6.2 fusion.43
  915.7 5.1 convert_bitcast_fusion.1
  920.8 6.9 all-to-all-start.1
  928.2 146.3 %all-to-all-done.1 = bf16[16,1,88,2048]{3,2,1,0:T(8,128)(2,1)} async-done(((bf16[16,1,88,2048]{3,2,1,0:T(8,128)(2,1)}), bf16[16,1,88,2048]{3,2,1,0:T(8,128)(2,1)}, u32[]{:S(2)}, u32[]{:S(2)}) %all-to-all-start.1) | async-done | bytes 5767200 | tf_op jit(solution)/shard_map/all_to_all | solution.py:221
  1074.5 14.3 %gather_fusion.1 = bf16[1280,2048]{1,0:T(8,128)(2,1)} fusion(bf16[1408,2048]{1,0:T(8,128)(2,1)} %bitcast.59, s32[2048]{0:T(1024)S(1)} %pad_clamp_fusion), kind=kCustom, calls=%fused_computation.1 | custom fusion | bytes 10490880 | tf_op jit(solution)/shard_map/gather | solution.py:222
  1088.8 9.5 reshape.754
  1098.3 8.7 multiply_reduce_fusion
  (262 shorter events, 149.0 us)
Async XLA Ops:
  6.5 909.1 %copy-start = (bf16[1,512,2048]{2,1,0:T(8,128)(2,1)S(1)}, bf16[1,512,2048]{2,1,0:T(8,128)(2,1)}, u32[]{:S(2)}) copy-start(bf16[1,512,2048]{2,1,0:T(8,128)(2,1)} %param.33) | copy-start | bytes 6291460
  6.5 105.7 %all-gather.7.cloned.1.call-start = ((), (), s32[]{:S(2)}) async-start(), calls=%async_computation.5 | async-start | bytes 2228224 | tf_op jit(solution)/shard_map/all_gather | solution.py:158
  7.3 199.8 %all-gather.5.cloned.1.call-start = ((), (), s32[]{:S(2)}) async-start(), calls=%async_computation.3 | async-start | bytes 8912896 | tf_op jit(solution)/shard_map/all_gather | solution.py:147
  11.3 748.0 %reduce-scatter.2.cloned.1.call-start = ((), (), s32[]{:S(2)}) async-start(), calls=%async_computation.4 | async-start | bytes 8912896 | tf_op jit(solution)/shard_map/reduce_scatter | solution.py:186
  329.2 2.1 copy-start.1
  340.1 3.4 copy-start.9
  515.0 3.4 copy-start.8
  520.4 1.9 copy-start.6
  611.9 1.0 copy-start.7
  621.6 0.7 copy-start.11
  621.6 1.1 copy-start.12
  621.6 137.7 %copy-start.2 = (bf16[1,128,2048]{2,1,0:T(8,128)(2,1)S(1)}, bf16[1,128,2048]{2,1,0:T(8,128)(2,1)}, u32[]{:S(2)}) copy-start(bf16[1,128,2048]{2,1,0:T(8,128)(2,1)} %param.19) | copy-start | bytes 1572868
  761.9 0.8 copy-start.4
  769.6 139.9 %copy-start.13 = (bf16[1,2048,1024]{2,1,0:T(8,128)(2,1)S(1)}, bf16[1,2048,1024]{2,1,0:T(8,128)(2,1)}, u32[]{:S(2)}) copy-start(bf16[1,2048,1024]{2,1,0:T(8,128)(2,1)} %param.32) | copy-start | bytes 12582916
  920.8 6.9 copy-start.5
  920.8 6.9 copy-start.10
  920.8 153.7 %all-to-all-start.1 = ((bf16[16,1,88,2048]{3,2,1,0:T(8,128)(2,1)}), bf16[16,1,88,2048]{3,2,1,0:T(8,128)(2,1)}, u32[]{:S(2)}, u32[]{:S(2)}) async-start(bf16[16,1,88,2048]{3,2,1,0:T(8,128)(2,1)} %convert_bitcast_fusion.1), calls=%async_computation.2 | async-start | bytes 11534336 | tf_op jit(solution)/shard_map/all_to_all | solution.py:221
  1098.3 8.7 copy-start.3
Sparse Core Ops, SparseCore 0:
  9.1 70.1 all-gather.6
  82.1 124.9 all-gather.4
  621.7 137.5 reduce-scatter.1
where the time goes:
time: 1130 us; the launch traced here: 1110 us
  waiting for transfers between devices  367 us (32%)
  blocking collectives  236 us (21%)
  matrix products  210 us (19%)
  other arithmetic  195 us (17%)
  local copies, waits for them, and re-layouts  84 us (7%)
  between operations  14.4 us (1%)
    another operation x4, other arithmetic, block_rule(): jax.scipy.linalg.solve_triangular(system, right_side, lower=True, unit_di...  159 us
    all_to_all x1, waiting for transfers between devices, on_device(): lax.all_to_all(result, 'expert', split_axis=0, concat_axis=0, tiled=True)  146 us
    all_to_all x1, blocking collectives, on_device(): lax.all_to_all(outgoing, 'expert', split_axis=0, concat_axis=0, tiled=True)  140 us
    reduce_scatter x1, waiting for transfers between devices, on_device(): lax.psum_scatter(head_products(head_out, out_columns).astype(jnp.bfloat16...  126 us
    all_gather x1, waiting for transfers between devices, on_device(): sequence = lax.all_gather(normed_own, 'expert', axis=0, tiled=True)  94.8 us
    dot_general x16, matrix products, one_block(): jnp.einsum('tq,qhc->thc', columns, main_piece[block_idx], preferred_eleme...  79.7 us
    all_gather x1, blocking collectives, on_device(): out_columns = lax.all_gather(out_weight, 'fsdp', axis=2, tiled=True)  38.7 us
    all_gather x1, blocking collectives, on_device(): gate_piece = lax.all_gather(gate_blocks, 'fsdp', axis=0, tiled=True)  30.9 us
  transfers between devices with their start and end apart: 4, of which 3 were waited for; matrix products, arithmetic and copies ran while one was open for 2% of the time, Pallas kernels for 0%

commit v1 on v0

v1 whole, which is shorter than its diff:
```python
import functools

import jax
import jax.numpy as jnp
from jax import lax
from jax.experimental import pallas as pl
from jax.experimental.pallas import tpu as pltpu
from jax.sharding import PartitionSpec as P

D = 2048
FF = 512
EXPERTS = 16

HD = 128
C = 128
PASSES = 3
f32 = jnp.float32
bf16 = jnp.bfloat16

def split(a):
    hi = a.astype(bf16)
    return hi, (a - hi.astype(f32)).astype(bf16)

def dg(a, b, dims):
    return lax.dot_general(a, b, (dims, ((), ())), preferred_element_type=f32)

NN = ((1,), (0,))
NT = ((1,), (1,))
TN = ((0,), (0,))

def mm(a, b, dims=NN, passes=3):
    if passes == 1:
        return dg(a.astype(bf16), b.astype(bf16), dims)
    ah, al = split(a); bh, bl = split(b)
    return dg(ah, bh, dims) + (dg(al, bh, dims) + dg(ah, bl, dims))

def prep_chunk(c, qkv_ref, gates_ref, docs_ref, win_ref, docc_ref, convw, rate):
    r0 = pl.multiple_of(c * C, C)
    docw = docc_ref[pl.ds(r0, C + 8), :]
    doc_col = docw[8:, :]
    parts = []
    for g in range(3):
        w = win_ref[pl.ds(r0, C + 8), g * HD:(g + 1) * HD]
        acc = w[8:, :] * convw[0:1, g * HD:(g + 1) * HD]
        for j in range(1, 4):
            keep = docw[8 - j:C + 8 - j, :] == doc_col
            acc = acc + jnp.where(keep, w[8 - j:C + 8 - j, :] * convw[j:j + 1, g * HD:(g + 1) * HD], 0.0)
        parts.append(acc * jax.nn.sigmoid(acc))
    q, k, v = parts
    q = q * (lax.rsqrt(jnp.sum(q * q, axis=1, keepdims=True) + 1e-6) * HD ** -0.5)
    k = k * lax.rsqrt(jnp.sum(k * k, axis=1, keepdims=True) + 1e-6)
    gates = gates_ref[pl.ds(r0, C), :]
    beta = jnp.broadcast_to(jax.nn.sigmoid(gates[:, 0:1]), (C, HD))
    d = gates[:, 1:2]
    sp = jnp.maximum(d, 0.0) + jnp.log1p(jnp.exp(-jnp.abs(d)))
    lg = jnp.broadcast_to(-rate * sp, (C, HD))
    row = lax.broadcasted_iota(jnp.int32, (C, C), 0)
    col = lax.broadcasted_iota(jnp.int32, (C, C), 1)
    low = (row >= col)
    tri = low.astype(bf16)
    h0 = lg.astype(bf16); r1 = lg - h0.astype(f32); h1 = r1.astype(bf16); h2 = (r1 - h1.astype(f32)).astype(bf16)
    cum = dg(tri, h0, NN) + (dg(tri, h1, NN) + dg(tri, h2, NN))
    doc_row = docs_ref[pl.ds(c, 1), :]
    keep = jnp.logical_and(low, doc_col == doc_row)
    gap = cum - cum.T
    decay = jnp.where(keep, jnp.exp(jnp.where(keep, gap, 0.0)), 0.0)
    prev = docw[7:8, :]
    start = jnp.where(doc_col == prev, jnp.exp(cum), 0.0)
    kk = mm(k, k, NT, PASSES)
    qk = mm(q, k, NT, PASSES) * decay
    L = jnp.where(row > col, beta * kk * decay, 0.0)
    eye = (row == col).astype(f32)
    T = eye - jnp.where((row >> 1) == (col >> 1), L, 0.0)
    s = 2
    while s < C:
        sh = s.bit_length() - 1
        m = jnp.logical_and((row >> (sh + 1)) == (col >> (sh + 1)), (row >> sh) != (col >> sh))
        Lm = jnp.where(m, L, 0.0)
        T = T - mm(T, mm(Lm, T, NN, PASSES), NN, PASSES)
        s *= 2
    rhs = jnp.concatenate([beta * v, beta * start * k], axis=1)
    UW = mm(T, rhs, NN, PASSES)
    kend = k * decay.T[:, C - 1:C]
    gend = start[C - 1:C, :]
    PUW = mm(qk, UW, NN, PASSES)
    KUW = mm(kend, UW, TN, PASSES)
    N = KUW[:, :HD]
    M = eye * gend - KUW[:, HD:]
    PU = PUW[:, :HD]
    Qp = start * q - PUW[:, HD:]
    return M, N, Qp, PU

def body(proj_ref, gates_ref, docs_ref, convw_ref, rate_ref, gain_ref, out_ref, win_ref, docc_ref, m_ref, n_ref, *, unroll):
    T_ = proj_ref.shape[0]
    nc = T_ // C
    win_ref[0:8, :] = jnp.zeros((8, 3 * HD), f32)
    docc_ref[0:8, :] = jnp.full((8, HD), -1.0, f32)
    convw = convw_ref[...]
    rate = rate_ref[0]
    def stage(c, _):
        r0 = pl.multiple_of(c * C, C)
        win_ref[pl.ds(pl.multiple_of(r0 + 8, 8), C), :] = proj_ref[pl.ds(r0, C), :3 * HD].astype(f32)
        docc_ref[pl.ds(pl.multiple_of(r0 + 8, 8), C), :] = jnp.broadcast_to(docs_ref[pl.ds(c, 1), :], (C, C)).T
        return 0
    lax.fori_loop(0, nc, stage, 0)
    def first(i, _):
        for u in range(unroll):
            c = i * unroll + u
            M, N, Qp, PU = prep_chunk(c, proj_ref, gates_ref, docs_ref, win_ref, docc_ref, convw, rate)
            m_ref[c, :C, :] = Qp
            m_ref[c, C:, :] = M
            n_ref[c, :C, :] = PU
            n_ref[c, C:, :] = N
        return 0
    lax.fori_loop(0, nc // unroll, first, 0)
    gain = gain_ref[...].astype(f32)
    def second(c, S):
        r0 = pl.multiple_of(c * C, C)
        both = mm(m_ref[c], S, NN, PASSES) + n_ref[c]
        o = both[:C, :]
        ms = jnp.mean(o * o, axis=1, keepdims=True)
        g = proj_ref[pl.ds(r0, C), 3 * HD:4 * HD].astype(f32)
        out_ref[pl.ds(r0, C), :] = (o * lax.rsqrt(ms + 1e-6) * gain * (g * jax.nn.sigmoid(g))).astype(bf16)
        return both[C:, :]
    lax.fori_loop(0, nc, second, jnp.zeros((HD, HD), f32))

def mixer_kernel(proj, gates, docs, convw, rate, gain, unroll=4):
    T_ = proj.shape[0]
    V = pl.BlockSpec(memory_space=pltpu.VMEM)
    return pl.pallas_call(
        functools.partial(body, unroll=unroll),
        out_shape=jax.ShapeDtypeStruct((T_, HD), bf16),
        in_specs=[V, V, V, V, pl.BlockSpec(memory_space=pltpu.SMEM), V],
        out_specs=V,
        scratch_shapes=[pltpu.VMEM((T_ + 8, 3 * HD), f32), pltpu.VMEM((T_ + 8, HD), f32),
                        pltpu.VMEM((T_ // C, 2 * C, HD), f32), pltpu.VMEM((T_ // C, 2 * C, HD), f32)],
        compiler_params=pltpu.CompilerParams(vmem_limit_bytes=48 * 1024 * 1024),
        name="delta_mixer",
    )(proj, gates, docs, convw, rate, gain)


def rms_scale(values, gain):
    mean_square = jnp.mean(values * values, axis=-1, keepdims=True)
    return values * lax.rsqrt(mean_square + 1e-06) * gain.astype(f32)


def on_device(tokens, doc_ids, route_ids, norm_gain, proj_weight, gating_weight, block_scale,
              conv_weight, decay_rate, head_gain, out_weight, moe_gain, router_weight,
              expert_in, expert_out):
    residual = tokens[0].astype(f32)
    normed = rms_scale(residual, norm_gain).astype(bf16)
    scale = jnp.repeat(block_scale[0, 0].astype(f32), HD)
    scaled = (proj_weight[:, 0, :].astype(f32) * scale[None, :]).astype(bf16)
    packed = jnp.concatenate([scaled, jnp.pad(gating_weight[:, :, 0], ((0, 0), (0, HD - 2)))], 1)
    sequence = lax.all_gather(normed, "expert", axis=0, tiled=True)
    weights = lax.all_gather(packed, "fsdp", axis=0, tiled=True)
    projected = jnp.dot(sequence, weights, preferred_element_type=f32)
    head_out = mixer_kernel(
        projected[:, :4 * HD].astype(bf16), projected[:, 4 * HD:],
        doc_ids[0].astype(f32).reshape(-1, C), conv_weight[0].astype(f32), decay_rate,
        head_gain.reshape(1, HD))
    out_full = lax.all_gather(lax.all_gather(out_weight[0], "fsdp", axis=1, tiled=True),
                              "expert", axis=0, tiled=True)
    tok = residual.shape[0]
    mine = lax.all_to_all(head_out.reshape(-1, tok, HD), "expert", split_axis=0, concat_axis=0, tiled=True)
    mine = jnp.swapaxes(mine, 0, 1).reshape(tok, D)
    mid = residual + jnp.dot(mine, out_full, preferred_element_type=f32)
    moe_in = rms_scale(mid, moe_gain).astype(bf16)
    logits = jnp.dot(moe_in, router_weight, preferred_element_type=f32)
    picked = (route_ids[0][:, :, None] == jnp.arange(EXPERTS, dtype=jnp.int32)).any(axis=1)
    raised = jnp.where(picked, jnp.exp(logits), 0.0)
    route_weight = raised / jnp.sum(raised, axis=1, keepdims=True)
    high = route_weight.astype(bf16)
    rest = (route_weight - high.astype(f32)).astype(bf16)
    sent = jnp.concatenate([moe_in, high, rest, jnp.zeros((tok, HD - 2 * EXPERTS), bf16)], 1)
    got = lax.all_gather(sent, "expert", axis=0, tiled=True)
    me = lax.axis_index("expert")
    lane = jnp.arange(HD)
    side = got[:, D:].astype(f32)
    weight = jnp.sum(jnp.where((lane == me) | (lane == me + EXPERTS), side, 0.0), axis=1, keepdims=True)
    gate_up = jnp.dot(got[:, :D], expert_in[0], preferred_element_type=f32)
    hidden = (jax.nn.silu(gate_up[:, :FF]) * gate_up[:, FF:]).astype(bf16)
    rows = (jnp.dot(hidden, expert_out[0], preferred_element_type=f32) * weight).astype(bf16)
    mixed = lax.psum_scatter(rows, "expert", scatter_dimension=0, tiled=True)
    return (mid + mixed.astype(f32)).astype(bf16)[None]


def solution(mesh):
    placed = (
        P("fsdp", "expert", None),
        P("fsdp", None),
        P("fsdp", "expert", None),
        P(),
        P("fsdp", "expert", None),
        P("fsdp", None, "expert"),
        P("fsdp", "expert", None),
        P("expert", None, None),
        P("expert"),
        P(),
        P("expert", None, "fsdp"),
        P(),
        P(),
        P("expert", None, None),
        P("expert", None, None),
    )
    return jax.shard_map(
        on_device, mesh=mesh, in_specs=placed, out_specs=P("fsdp", "expert", None), check_vma=False
    )
```

time: 1130 us -> 615 us (0.54)
  the two profiles are of different devices: /device:TPU:79 before, /device:TPU:224 now
where the time goes in v1:
time: 615 us; the launch traced here: 608 us
  waiting for transfers between devices  435 us (71%)
  Pallas kernels  51 us (8%)
  blocking collectives  47.8 us (8%)
  matrix products  34.4 us (6%)
  between operations  14 us (2%)
  other arithmetic  11.2 us (2%)
  starting transfers between devices  8.84 us (1%)
  local copies, waits for them, and re-layouts  6.23 us (1%)
    reduce_scatter x1, waiting for transfers between devices, on_device(): mixed = lax.psum_scatter(rows, 'expert', scatter_dimension=0, tiled=True)  143 us
    all_gather x1, waiting for transfers between devices, on_device(): sequence = lax.all_gather(normed, 'expert', axis=0, tiled=True)  105 us
    all_gather x1, waiting for transfers between devices, on_device(): got = lax.all_gather(sent, 'expert', axis=0, tiled=True)  102 us
    pallas_call x1, Pallas kernels, mixer_kernel(): pl.pallas_call(functools.partial(body, unroll=unroll), out_shape=jax.Shap...  51 us
    all_gather x1, waiting for transfers between devices, on_device(): lax.all_gather(lax.all_gather(out_weight[0], 'fsdp', axis=1, tiled=True),...  49.2 us
    all_gather x1, blocking collectives, on_device(): lax.all_gather(out_weight[0], 'fsdp', axis=1, tiled=True)  47.8 us
    all_gather x1, waiting for transfers between devices, on_device(): weights = lax.all_gather(packed, 'fsdp', axis=0, tiled=True)  35.9 us
    dot_general x1, matrix products, on_device(): gate_up = jnp.dot(got[:, :D], expert_in[0], preferred_element_type=f32)  12.5 us
  transfers between devices with their start and end apart: 6, of which 5 were waited for; matrix products, arithmetic and copies ran while one was open for 3% of the time, Pallas kernels for 8%

profile of v1, /device:TPU:224, one launch (start us, length us, event | category | flops | bytes accessed | tf_op | source)
XLA Modules:
  0.0 608.4 jit_solution(12108674864449990664)
XLA Ops:
  6.5 0.8 bitcast_convert_fusion.1
  7.3 0.1 broadcast_bitcast_fusion
  7.4 0.8 copy.32
  8.2 0.9 fusion.18
  9.1 0.7 fusion.19
  9.8 0.0 all-gather.9.cloned.1.call-update
  9.8 0.0 all-gather.7.cloned.1.call-start
  9.9 0.7 convert_element_type.74
  10.6 1.2 fusion.13
  11.8 2.0 fusion.15
  13.8 0.0 all-gather.7.cloned.1.call-update
  13.9 0.0 all-gather.13.cloned.1.call-start
  13.9 47.8 %all-gather = bf16[1,128,2048]{2,1,0:T(8,128)(2,1)} all-gather(bf16[1,128,128]{2,1,0:T(8,128)(2,1)} %param.25), channel_id=2, replica_groups=mesh['fsdp'=16,'expert'=16] {'fsdp'}, dimensions={2}, use_global_device_ids=true | all-gather | bytes 557056 | tf_op jit(solution)/shard_map/all_gather | solution.py:162
  61.7 0.0 all-gather.13.cloned.1.call-update
  62.4 0.7 convert_element_type.81
  63.1 0.7 bitcast_convert_fusion.convw_ref
  63.8 35.9 %all-gather.9.cloned.1.call-done = bf16[2048,640]{1,0:T(8,128)(2,1)} async-done(((bf16[128,640]{1,0:T(8,128)(2,1)}), bf16[2048,640]{1,0:T(8,128)(2,1)}) %all-gather.9.cloned.1.call-update) | async-done | bytes 2621456 | tf_op jit(solution)/shard_map/all_gather | solution.py:156
  99.7 104.6 %all-gather.7.cloned.1.call-done = bf16[2048,2048]{1,0:T(8,128)(2,1)} async-done(((bf16[128,2048]{1,0:T(8,128)(2,1)}), bf16[2048,2048]{1,0:T(8,128)(2,1)}) %all-gather.7.cloned.1.call-update) | async-done | bytes 8388624 | tf_op jit(solution)/shard_map/all_gather | solution.py:155
  204.3 9.9 %fusion.24 = f32[2048,640]{1,0:T(8,128)S(1)} fusion(bf16[2048,2048]{1,0:T(8,128)(2,1)} %all-gather.7.cloned.1.call-done, bf16[2048,640]{1,0:T(8,128)(2,1)} %all-gather.9.cloned.1.call-done), kind=kOutput, calls=%fused_computation.43 | convolution fusion | flops 5368709120 | bytes 16252928 | tf_op jit(solution)/shard_map/dot_general | solution.py:157
  214.2 0.0 copy-start.1
  214.2 0.1 slice.26.gates_ref
  214.3 0.0 copy-start.5
  214.3 0.0 copy-start.6
  214.3 0.2 slice.41.proj_ref
  214.5 0.3 copy-done.1
  214.8 51.0 %delta_mixer.1 = bf16[2048,128]{1,0:T(8,128)(2,1)S(1)} custom-call(bf16[2048,512]{1,0:T(8,128)(2,1)S(1)} %slice.41.proj_ref, f32[2048,128]{1,0:T(8,128)S(1)} %slice.26.gates_ref, f32[16,128]{1,0:T(8,128)S(1)} %bitcast.47, f32[4,384]{1,0:T(4,128)S(1)} %bitcast_convert_fusion.convw_ref, f32[1]{0:T(128)S(6)} %copy.35.rate_ref, bf16[1,128]{1,0:T(2,128)(2,1)S(1)} %bitcast.48), custom_call_target="tpu_custom_call" | custom-call | tf_op jit(solution)/shard_map/delta_mixer/pallas_call | solution.py:130
  265.8 1.0 copy.28
  266.8 8.5 %all-to-all-start = ((bf16[16,128,128]{1,2,0:T(8,128)(2,1)}), bf16[16,128,128]{1,2,0:T(8,128)(2,1)S(1)}, u32[]{:S(2)}, u32[]{:S(2)}) async-start(bf16[16,128,128]{1,2,0:T(8,128)(2,1)} %copy.28), calls=%async_computation | async-start | bytes 1048576 | tf_op jit(solution)/shard_map/all_to_all | solution.py:165
  275.3 0.0 all-gather.11.cloned.1.call-start
  275.4 49.2 %all-gather.13.cloned.1.call-done = bf16[1,2048,2048]{2,1,0:T(8,128)(2,1)} async-done(((bf16[1,128,2048]{2,1,0:T(8,128)(2,1)}), bf16[1,2048,2048]{2,1,0:T(8,128)(2,1)}) %all-gather.13.cloned.1.call-update) | async-done | bytes 8388624 | tf_op jit(solution)/shard_map/all_gather | solution.py:162
  324.6 0.8 copy-done.3
  325.4 5.0 multiply_reduce_fusion
  330.4 0.2 multiply_convert_fusion.1
  330.5 0.0 copy-start.2
  330.5 0.8 copy-done.2
  331.3 0.3 fusion.23
  331.6 0.1 copy.30
  331.7 0.1 copy.29
  331.9 1.9 concatenate.7
  333.8 0.0 all-gather.11.cloned.1.call-update
  333.8 0.2 reduce-scatter.2.cloned.1.call-start
  334.1 102.1 %all-gather.11.cloned.1.call-done = bf16[2048,2176]{1,0:T(8,128)(2,1)} async-done(((bf16[128,2176]{1,0:T(8,128)(2,1)}), bf16[2048,2176]{1,0:T(8,128)(2,1)}) %all-gather.11.cloned.1.call-update) | async-done | bytes 8912912 | tf_op jit(solution)/shard_map/all_gather | solution.py:176
  436.1 1.3 select_reduce_fusion
  437.4 12.5 %fusion = f32[2048,1024]{1,0:T(8,128)S(1)} fusion(bf16[2048,2176]{1,0:T(8,128)(2,1)} %all-gather.11.cloned.1.call-done, bf16[1,2048,1024]{2,1,0:T(8,128)(2,1)} %param.28), kind=kOutput, calls=%fused_computation.1 | convolution fusion | flops 8589934592 | bytes 20971520 | tf_op jit(solution)/shard_map/dot_general | solution.py:181
  449.9 6.9 %multiply_convert_fusion = bf16[2048,2048]{1,0:T(8,128)(2,1)} fusion(f32[2048]{0:T(1024)S(1)} %select_reduce_fusion, f32[2048,1024]{1,0:T(8,128)S(1)} %fusion, bf16[1,512,2048]{2,1,0:T(8,128)(2,1)S(1)} %copy-done), kind=kOutput, calls=%fused_computation | convolution fusion | flops 4309647360 | bytes 18882560 | tf_op jit(solution)/shard_map/dot_general | solution.py:183
  456.8 0.0 reduce-scatter.2.cloned.1.call-update
  456.8 143.1 %reduce-scatter.2.cloned.1.call-done = bf16[128,2048]{1,0:T(8,128)(2,1)} async-done(((bf16[2048,2048]{1,0:T(8,128)(2,1)}), bf16[128,2048]{1,0:T(8,128)(2,1)}) %reduce-scatter.2.cloned.1.call-update) | async-done | bytes 524304 | tf_op jit(solution)/shard_map/reduce_scatter | solution.py:184
  599.9 1.9 fusion.16
  (17 shorter events, 0.1 us)
Async XLA Ops:
  6.5 443.3 %copy-start = (bf16[1,512,2048]{2,1,0:T(8,128)(2,1)S(1)}, bf16[1,512,2048]{2,1,0:T(8,128)(2,1)}, u32[]{:S(2)}) copy-start(bf16[1,512,2048]{2,1,0:T(8,128)(2,1)} %param.29) | copy-start | bytes 6291460
  6.5 93.1 %all-gather.9.cloned.1.call-start = ((), (), s32[]{:S(2)}) async-start(), calls=%async_computation.3 | async-start | bytes 2785280 | tf_op jit(solution)/shard_map/all_gather | solution.py:156
  9.8 194.5 %all-gather.7.cloned.1.call-start = ((), (), s32[]{:S(2)}) async-start(), calls=%async_computation.2 | async-start | bytes 8912896 | tf_op jit(solution)/shard_map/all_gather | solution.py:155
  13.9 310.7 %all-gather.13.cloned.1.call-start = ((), (), s32[]{:S(2)}) async-start(), calls=%async_computation.6 | async-start | bytes 8912896 | tf_op jit(solution)/shard_map/all_gather | solution.py:162
  214.2 0.7 copy-start.1
  214.3 61.1 %copy-start.5 = (s32[1,128,10]{1,0,2:T(1,128)S(1)}, s32[1,128,10]{1,0,2:T(1,128)}, u32[]{:S(2)}) copy-start(s32[1,128,10]{1,0,2:T(1,128)} %param.17) | copy-start | bytes 15364
  214.3 61.1 %copy-start.6 = (bf16[2048]{0:T(1024)(128)(2,1)S(1)}, bf16[2048]{0:T(1024)(128)(2,1)}, u32[]{:S(2)}) copy-start(bf16[2048]{0:T(1024)(128)(2,1)} %param.26) | copy-start | bytes 12292
  266.8 57.8 %all-to-all-start = ((bf16[16,128,128]{1,2,0:T(8,128)(2,1)}), bf16[16,128,128]{1,2,0:T(8,128)(2,1)S(1)}, u32[]{:S(2)}, u32[]{:S(2)}) async-start(bf16[16,128,128]{1,2,0:T(8,128)(2,1)} %copy.28), calls=%async_computation | async-start | bytes 1048576 | tf_op jit(solution)/shard_map/all_to_all | solution.py:165
  275.3 160.8 %all-gather.11.cloned.1.call-start = ((), (), s32[]{:S(2)}) async-start(), calls=%async_computation.4 | async-start | bytes 9469952 | tf_op jit(solution)/shard_map/all_gather | solution.py:176
  324.6 0.8 copy-start.3
  325.4 6.0 copy-start.4
  330.5 0.8 copy-start.2
  333.8 266.1 %reduce-scatter.2.cloned.1.call-start = ((), (), s32[]{:S(2)}) async-start(), calls=%async_computation.5 | async-start | bytes 8912896 | tf_op jit(solution)/shard_map/reduce_scatter | solution.py:184
Sparse Core Ops, SparseCore 0:
  10.0 89.6 all-gather.8
  102.4 101.8 all-gather.6
  207.1 117.4 all-gather.12
  333.9 102.1 all-gather.10
  456.9 142.9 reduce-scatter.1

commit v2 on v1

--- a/solution.py
+++ b/solution.py
@@ -10,6 +10,7 @@
 D = 2048
 FF = 512
 EXPERTS = 16
+MESH = pl.DeviceIdType.MESH
 
 HD = 128
 C = 128
@@ -144,19 +145,379 @@
     return values * lax.rsqrt(mean_square + 1e-06) * gain.astype(f32)
 
 
+class Place:
+    def __init__(self):
+        e = lax.axis_index("expert")
+        self.e = e
+        self.z, self.x, self.c = e // 8, (e // 2) % 4, e % 2
+
+    def at(self, zz, dx, cc=0):
+        return ((self.z + zz) % 2 * 4 + (self.x + dx) % 4) * 2 + (self.c + cc) % 2
+
+    def pair(self, zz, dx):
+        return ((self.z + zz) % 2 * 4 + (self.x + dx) % 4) * 2
+
+    def neighbours(self):
+        return [{"expert": self.at(*r)} for r in ((0, 1), (0, 3), (1, 0), (0, 0, 1))]
+
+
+def greet(peers):
+    barrier = pltpu.get_barrier_semaphore()
+    for peer in peers:
+        pl.semaphore_signal(barrier, inc=1, device_id=peer, device_id_type=MESH)
+    pl.semaphore_wait(barrier, len(peers))
+
+
+class Copies:
+    def __init__(self, send, recv):
+        self.send, self.recv, self.sent = send, recv, []
+
+    def make(self, i, src, dst, peer):
+        return pltpu.make_async_remote_copy(
+            src_ref=src, dst_ref=dst, send_sem=self.send.at[i], recv_sem=self.recv.at[i],
+            device_id=peer, device_id_type=MESH)
+
+    def go(self, i, src, dst, peer):
+        copy = self.make(i, src, dst, peer)
+        copy.start()
+        self.sent.append(copy)
+
+    def arrive(self, i, dst, peer):
+        self.make(i, dst, dst, peer).wait_recv()
+
+    def finish(self):
+        for copy in self.sent:
+            copy.wait_send()
+
+
+GATHER_COPIES = 30
+
+
+class Gather:
+    def __init__(self, full, copies, place, base=0):
+        self.full, self.copies, self.place, self.base = full, copies, place, base
+        self.half = full.shape[1] // 2
+
+    def ref(self, zz, dx, h, cc=0):
+        return self.full.at[self.place.at(zz, dx, cc), pl.ds(h * self.half, self.half)]
+
+    def peer(self, *r):
+        return {"expert": self.place.at(*r)}
+
+    def go(self, n, zz, dx, h, to):
+        block = self.ref(zz, dx, h)
+        self.copies.go(self.base + n, block, block, self.peer(*to))
+
+    def swap(self, zz, dx, h):
+        self.go(14 + (zz * 4 + dx) * 2 + h, zz, dx, h, (0, 0, 1))
+
+    def take(self, n, zz, dx, h):
+        self.copies.arrive(self.base + n, self.ref(zz, dx, h), self.peer(0, 1))
+        self.swap(zz, dx, h)
+
+    def swapped(self, zz, dx):
+        for h in range(2):
+            self.copies.arrive(self.base + 14 + (zz * 4 + dx) * 2 + h, self.ref(zz, dx, h, 1), self.peer(0, 0, 1))
+
+    def plus(self, zz, h):
+        self.go(2 + zz * 2 + h, zz, 0, h, (0, 1))
+
+    def minus(self, zz, h):
+        self.go(6 + zz * 2 + h, zz, 0, h, (0, 3))
+
+    def begin(self):
+        for h in range(2):
+            self.go(h, 0, 0, h, (1, 0))
+            self.plus(0, h)
+            self.minus(0, 1 - h)
+        self.swap(0, 0, 0)
+        self.swap(0, 0, 1)
+
+    def from_x(self, zz):
+        self.take(2 + zz * 2, zz, 3, 0)
+        self.go(10 + zz, zz, 3, 0, (0, 1))
+        self.take(6 + zz * 2 + 1, zz, 1, 1)
+        self.go(12 + zz, zz, 1, 1, (0, 3))
+        self.take(2 + zz * 2 + 1, zz, 3, 1)
+        self.take(6 + zz * 2, zz, 1, 0)
+
+    def from_z(self, h):
+        self.take(h, 1, 0, h)
+        self.plus(1, h)
+        self.minus(1, h)
+
+    def from_far(self, zz):
+        self.take(10 + zz, zz, 2, 0)
+        self.take(12 + zz, zz, 2, 1)
+
+
+def project_kernel(tok_ref, gain_ref, pack_ref, proj_ref, gate_ref, full, w, send, recv, *, wide):
+    place = Place()
+    fsdp = lax.axis_index("fsdp")
+    y, zl = fsdp // 4, fsdp % 4
+    tok = tok_ref.shape[0]
+    rows = pack_ref.shape[0]
+
+    def line(dy, d):
+        return (y + dy) % 4 * 4 + (zl + d) % 4
+
+    full[place.e] = rms_scale(tok_ref[...].astype(f32), gain_ref[...]).astype(bf16)
+    w[fsdp] = pack_ref[...]
+    greet(place.neighbours() + [{"fsdp": line(*r)} for r in ((1, 0), (3, 0), (0, 1), (0, 2), (0, 3))])
+    copies = Copies(send, recv)
+    gather = Gather(full, copies, place)
+    base = GATHER_COPIES
+    half = rows // 2
+
+    def shard(dy, d, h=None):
+        slot = w.at[line(dy, (4 - d) % 4)]
+        return slot if h is None else slot.at[pl.ds(h * half, half)]
+
+    def send_shard(n, ref, peer):
+        copies.go(base + n, ref, ref, {"fsdp": peer})
+
+    def both(d):
+        send_shard(3 + d, shard(0, d), line(1, 0))
+        send_shard(7 + d, shard(0, d), line(3, 0))
+
+    def along_z(d):
+        copies.arrive(base + d - 1, shard(0, d), {"fsdp": line(0, d)})
+        both(d)
+
+    def along_y(d):
+        copies.arrive(base + 3 + d, shard(3, d), {"fsdp": line(3, 0)})
+        send_shard(11 + d, shard(3, d, 0), line(1, 0))
+        copies.arrive(base + 7 + d, shard(1, d), {"fsdp": line(1, 0)})
+        send_shard(15 + d, shard(1, d, 1), line(3, 0))
+
+    def far_y(d):
+        copies.arrive(base + 11 + d, shard(2, d, 0), {"fsdp": line(3, 0)})
+        copies.arrive(base + 15 + d, shard(2, d, 1), {"fsdp": line(1, 0)})
+
+    def project(zz, dx):
+        gather.swapped(zz, dx)
+        slot = place.pair(zz, dx)
+        x = full[pl.ds(slot, 2)].reshape(2 * tok, full.shape[2])
+        at = pl.ds(pl.multiple_of(slot * tok, 2 * tok), 2 * tok)
+        for n in range(0, wide, 256):
+            proj_ref[at, n:n + 256] = dg(x, w[:, :, n:n + 256].reshape(16 * rows, 256), NN).astype(bf16)
+        gate_ref[at, :] = dg(x, w[:, :, wide:].reshape(16 * rows, HD), NN)
+
+    for d in range(1, 4):
+        send_shard(d - 1, w.at[fsdp], line(0, d))
+    both(0)
+    gather.begin()
+    for d in range(1, 4):
+        along_z(d)
+    gather.from_x(0)
+    along_y(0)
+    gather.from_z(0)
+    along_y(1)
+    gather.from_z(1)
+    along_y(2)
+    gather.from_far(0)
+    along_y(3)
+    for d in range(4):
+        far_y(d)
+    project(0, 0)
+    project(0, 3)
+    gather.from_x(1)
+    project(0, 1)
+    project(0, 2)
+    project(1, 0)
+    gather.from_far(1)
+    project(1, 3)
+    project(1, 1)
+    project(1, 2)
+    copies.finish()
+
+
+def project_call(tokens, gain, packed):
+    tok, width = tokens.shape
+    rows, cols = packed.shape
+    wide = cols - HD
+    V = pl.BlockSpec(memory_space=pltpu.VMEM)
+    count = GATHER_COPIES + 19
+    return pl.pallas_call(
+        functools.partial(project_kernel, wide=wide),
+        out_shape=(jax.ShapeDtypeStruct((16 * tok, wide), bf16), jax.ShapeDtypeStruct((16 * tok, HD), f32)),
+        in_specs=[V] * 3,
+        out_specs=(V, V),
+        scratch_shapes=[pltpu.VMEM((16, tok, width), bf16), pltpu.VMEM((16, rows, cols), bf16),
+                        pltpu.SemaphoreType.DMA((count,)), pltpu.SemaphoreType.DMA((count,))],
+        compiler_params=pltpu.CompilerParams(collective_id=0, has_side_effects=True,
+                                             vmem_limit_bytes=48 * 1024 * 1024),
+        name="gather_project",
+    )(tokens, gain, packed)
+
+
+def add_rows(dst, sources, first, count):
+    def step(i, _):
+        at = pl.ds(pl.multiple_of(first + i * 16, 16), 16)
+        total = dst[at, :].astype(f32)
+        for source in sources:
+            total = total + source[at, :].astype(f32)
+        dst[at, :] = total.astype(bf16)
+        return 0
+    lax.fori_loop(0, count // 16, step, 0)
+
+
+def expert_kernel(sent_ref, mid_ref, ein_ref, eout_ref, out_ref, full, y, kin, ap, am, bp, bm, zb,
+                  win, wout, hid, send, recv, load):
+    place = Place()
+    tok, width = mid_ref.shape
+    half = tok // 2
+    ff = wout.shape[0]
+    loads = [pltpu.make_async_copy(ein_ref, win, load.at[0]), pltpu.make_async_copy(eout_ref, wout, load.at[1])]
+    for copy in loads:
+        copy.start()
+    full[place.e] = sent_ref[...]
+    greet(place.neighbours())
+    copies = Copies(send, recv)
+    gather = Gather(full, copies, place)
+    gather.begin()
+    for copy in loads:
+        copy.wait()
+    base = GATHER_COPIES
+    plus, minus = {"expert": place.at(0, 1)}, {"expert": place.at(0, 3)}
+    over, twin = {"expert": place.at(1, 0)}, {"expert": place.at(0, 0, 1)}
+    nf, nd = min(256, ff), min(256, width)
+
+    def compute(zz, dx):
+        gather.swapped(zz, dx)
+        slot = place.pair(zz, dx)
+        both = pl.ds(slot, 2)
+        lane = lax.broadcasted_iota(jnp.int32, (2 * tok, HD), 1)
+        side = full[both, :, width:].reshape(2 * tok, HD).astype(f32)
+        hit = jnp.logical_or(lane == place.e, lane == place.e + 16)
+        weight = jnp.sum(jnp.where(hit, side, 0.0), axis=1, keepdims=True)
+
+        def inner(j, _):
+            x = full[both, :, :width].reshape(2 * tok, width)
+            g = dg(x, win[:, pl.ds(pl.multiple_of(j * nf, nf), nf)], NN)
+            u = dg(x, win[:, pl.ds(pl.multiple_of(ff + j * nf, nf), nf)], NN)
+            hid[:, pl.ds(pl.multiple_of(j * nf, nf), nf)] = (g * jax.nn.sigmoid(g) * u).astype(bf16)
+            return 0
+        lax.fori_loop(0, ff // nf, inner, 0)
+
+        def outer(j, _):
+            cols = pl.ds(pl.multiple_of(j * nd, nd), nd)
+            out = dg(hid[...], wout[:, cols], NN) * weight
+            y[both, :, cols] = out.astype(bf16).reshape(2, tok, nd)
+            return 0
+        lax.fori_loop(0, width // nd, outer, 0)
+        n = base + zz * 4 + dx
+        copies.go(n, y.at[place.at(zz, dx, 1)], kin.at[zz * 4 + dx], twin)
+
+    def own(zz, dx):
+        return y.at[place.at(zz, dx)]
+
+    def chip_sum(zz, dx):
+        copies.arrive(base + zz * 4 + dx, kin.at[zz * 4 + dx], twin)
+        add_rows(own(zz, dx), [kin.at[zz * 4 + dx]], 0, tok)
+
+    low, high = pl.ds(0, half), pl.ds(half, half)
+
+    def far(zz):
+        chip_sum(zz, 2)
+        copies.go(base + 8 + zz, own(zz, 2).at[low], ap.at[zz], plus)
+        copies.go(base + 10 + zz, own(zz, 2).at[high], am.at[zz], minus)
+
+    def near(zz):
+        chip_sum(zz, 1)
+        copies.go(base + 12 + zz, own(zz, 1).at[high], bp.at[zz, high], plus)
+        chip_sum(zz, 3)
+        copies.go(base + 14 + zz, own(zz, 3).at[low], bm.at[zz, low], minus)
+
+    def relay(zz):
+        copies.arrive(base + 8 + zz, ap.at[zz], minus)
+        add_rows(own(zz, 1).at[low], [ap.at[zz]], 0, half)
+        copies.go(base + 16 + zz, own(zz, 1).at[low], bp.at[zz, low], plus)
+        copies.arrive(base + 10 + zz, am.at[zz], plus)
+        add_rows(own(zz, 3).at[high], [am.at[zz]], 0, half)
+        copies.go(base + 18 + zz, own(zz, 3).at[high], bm.at[zz, high], minus)
+
+    def settle(zz, h):
+        if h == 0:
+            copies.arrive(base + 14 + zz, bm.at[zz, low], plus)
+            copies.arrive(base + 16 + zz, bp.at[zz, low], minus)
+        else:
+            copies.arrive(base + 12 + zz, bp.at[zz, high], minus)
+            copies.arrive(base + 18 + zz, bm.at[zz, high], plus)
+
+    compute(0, 0)
+    gather.from_x(0)
+    compute(0, 3)
+    gather.from_z(0)
+    compute(0, 1)
+    gather.from_z(1)
+    gather.from_far(0)
+    compute(0, 2)
+    gather.from_x(1)
+    far(0)
+    compute(1, 0)
+    near(0)
+    gather.from_far(1)
+    compute(1, 3)
+    relay(0)
+    compute(1, 1)
+    compute(1, 2)
+    far(1)
+    near(1)
+    relay(1)
+    chip_sum(1, 0)
+    for h, part in ((0, low), (1, high)):
+        settle(1, h)
+        add_rows(own(1, 0), [bp.at[1], bm.at[1]], h * half, half)
+        copies.go(base + 20 + h, own(1, 0).at[part], zb.at[part], over)
+    chip_sum(0, 0)
+    for h, part in ((0, low), (1, high)):
+        settle(0, h)
+        copies.arrive(base + 20 + h, zb.at[part], over)
+
+        def last(i, _):
+            at = pl.ds(pl.multiple_of(h * half + i * 16, 16), 16)
+            total = mid_ref[at, :]
+            for source in (own(0, 0), bp.at[0], bm.at[0], zb):
+                total = total + source[at, :].astype(f32)
+            out_ref[at, :] = total.astype(bf16)
+            return 0
+        lax.fori_loop(0, half // 16, last, 0)
+    copies.finish()
+
+
+def expert_call(sent, mid, expert_in, expert_out):
+    tok, width = mid.shape
+    ff = expert_out.shape[0]
+    V, A = pl.BlockSpec(memory_space=pltpu.VMEM), pl.BlockSpec(memory_space=pl.ANY)
+    count = GATHER_COPIES + 22
+    vm = lambda *s: pltpu.VMEM(s, bf16)
+    return pl.pallas_call(
+        expert_kernel,
+        out_shape=jax.ShapeDtypeStruct((tok, width), bf16),
+        in_specs=[V, V, A, A],
+        out_specs=V,
+        scratch_shapes=[vm(16, tok, width + HD), vm(16, tok, width), vm(8, tok, width),
+                        vm(2, tok // 2, width), vm(2, tok // 2, width), vm(2, tok, width), vm(2, tok, width),
+                        vm(tok, width), vm(width, 2 * ff), vm(ff, width), vm(2 * tok, ff),
+                        pltpu.SemaphoreType.DMA((count,)), pltpu.SemaphoreType.DMA((count,)),
+                        pltpu.SemaphoreType.DMA((2,))],
+        compiler_params=pltpu.CompilerParams(collective_id=1, has_side_effects=True,
+                                             vmem_limit_bytes=52 * 1024 * 1024),
+        name="expert_exchange",
+    )(sent, mid, expert_in, expert_out)
+
+
 def on_device(tokens, doc_ids, route_ids, norm_gain, proj_weight, gating_weight, block_scale,
               conv_weight, decay_rate, head_gain, out_weight, moe_gain, router_weight,
               expert_in, expert_out):
     residual = tokens[0].astype(f32)
-    normed = rms_scale(residual, norm_gain).astype(bf16)
     scale = jnp.repeat(block_scale[0, 0].astype(f32), HD)
     scaled = (proj_weight[:, 0, :].astype(f32) * scale[None, :]).astype(bf16)
     packed = jnp.concatenate([scaled, jnp.pad(gating_weight[:, :, 0], ((0, 0), (0, HD - 2)))], 1)
-    sequence = lax.all_gather(normed, "expert", axis=0, tiled=True)
-    weights = lax.all_gather(packed, "fsdp", axis=0, tiled=True)
-    projected = jnp.dot(sequence, weights, preferred_element_type=f32)
+    projected, gates = project_call(tokens[0], norm_gain.reshape(1, D), packed)
     head_out = mixer_kernel(
-        projected[:, :4 * HD].astype(bf16), projected[:, 4 * HD:],
+        projected, gates,
         doc_ids[0].astype(f32).reshape(-1, C), conv_weight[0].astype(f32), decay_rate,
         head_gain.reshape(1, HD))
     out_full = lax.all_gather(lax.all_gather(out_weight[0], "fsdp", axis=1, tiled=True),
@@ -173,16 +534,7 @@
     high = route_weight.astype(bf16)
     rest = (route_weight - high.astype(f32)).astype(bf16)
     sent = jnp.concatenate([moe_in, high, rest, jnp.zeros((tok, HD - 2 * EXPERTS), bf16)], 1)
-    got = lax.all_gather(sent, "expert", axis=0, tiled=True)
-    me = lax.axis_index("expert")
-    lane = jnp.arange(HD)
-    side = got[:, D:].astype(f32)
-    weight = jnp.sum(jnp.where((lane == me) | (lane == me + EXPERTS), side, 0.0), axis=1, keepdims=True)
-    gate_up = jnp.dot(got[:, :D], expert_in[0], preferred_element_type=f32)
-    hidden = (jax.nn.silu(gate_up[:, :FF]) * gate_up[:, FF:]).astype(bf16)
-    rows = (jnp.dot(hidden, expert_out[0], preferred_element_type=f32) * weight).astype(bf16)
-    mixed = lax.psum_scatter(rows, "expert", scatter_dimension=0, tiled=True)
-    return (mid + mixed.astype(f32)).astype(bf16)[None]
+    return expert_call(sent, mid, expert_in[0], expert_out[0])[None]
 
 
 def solution(mesh):

time: 615 us -> 337 us (0.55)
  the two profiles are of different devices: /device:TPU:224 before, /device:TPU:39 now
where the time goes in v2:
time: 337 us
  Pallas kernels  236 us (70%)
  blocking collectives  38.2 us (11%)
  starting transfers between devices  16.7 us (5%)
  waiting for transfers between devices  16.3 us (5%)
  between operations  14.2 us (4%)
  local copies, waits for them, and re-layouts  6.16 us (2%)
  matrix products  5.1 us (2%)
  other arithmetic  3.97 us (1%)
    pallas_call x1, Pallas kernels, expert_call(): pl.pallas_call(expert_kernel, out_shape=jax.ShapeDtypeStruct((tok, width)...  102 us
    pallas_call x1, Pallas kernels, project_call(): pl.pallas_call(functools.partial(project_kernel, wide=wide), out_shape=(j...  82.7 us
    pallas_call x1, Pallas kernels, mixer_kernel(): pl.pallas_call(functools.partial(body, unroll=unroll), out_shape=jax.Shap...  51 us
    all_gather x1, blocking collectives, on_device(): lax.all_gather(out_weight[0], 'fsdp', axis=1, tiled=True)  38.2 us
    all_to_all x1, starting transfers between devices, on_device(): lax.all_to_all(head_out.reshape(-1, tok, HD), 'expert', split_axis=0, con...  16.7 us
    all_to_all x1, waiting for transfers between devices, on_device(): lax.all_to_all(head_out.reshape(-1, tok, HD), 'expert', split_axis=0, con...  16.3 us
  transfers between devices with their start and end apart: 2, of which 1 were waited for; matrix products, arithmetic and copies ran while one was open for 2% of the time, Pallas kernels for 40%

profile of v2, /device:TPU:39, one launch (start us, length us, event | category | flops | bytes accessed | tf_op | source)
XLA Modules:
  0.0 336.5 jit_solution(14706605766551349560)
XLA Ops:
  6.5 0.0 copy-start
  6.5 0.0 copy-start.2
  6.5 0.0 all-gather.4.cloned.1.call-start
  6.5 38.2 %all-gather = bf16[1,128,2048]{2,1,0:T(8,128)(2,1)} all-gather(bf16[1,128,128]{2,1,0:T(8,128)(2,1)} %param.25), channel_id=2, replica_groups=mesh['fsdp'=16,'expert'=16] {'fsdp'}, dimensions={2}, use_global_device_ids=true | all-gather | bytes 557056 | tf_op jit(solution)/shard_map/all_gather | solution.py:523
  44.7 0.0 all-gather.4.cloned.1.call-update
  44.7 0.8 copy.27
  45.5 0.7 reshape.33.gain_ref
  46.2 0.7 convert_element_type.53
  47.6 0.7 bitcast_convert_fusion.1
  48.2 0.1 broadcast_bitcast_fusion
  48.3 0.9 fusion.7
  49.3 0.0 copy-start.1
  49.3 1.0 copy-done.1
  50.3 82.7 %gather_project.1 = (bf16[2048,512]{1,0:T(8,128)(2,1)S(1)}, f32[2048,128]{1,0:T(8,128)S(1)}) custom-call(bf16[128,2048]{1,0:T(8,128)(2,1)S(1)} %bitcast.36, bf16[1,2048]{1,0:T(2,128)(2,1)S(1)} %reshape.33.gain_ref, bf16[128,640]{1,0:T(8,128)(2,1)S(1)} %fusion.8.pack_ref), custom_call_target="tpu_custom_call" | custom-call | tf_op jit(solution)/shard_map/gather_project/pallas_call | solution.py:341
  133.0 0.7 bitcast_convert_fusion.convw_ref
  133.7 0.0 copy-start.3
  133.7 0.7 copy-done.3
  134.3 51.0 %delta_mixer.1 = bf16[2048,128]{1,0:T(8,128)(2,1)S(1)} custom-call(bf16[2048,512]{1,0:T(8,128)(2,1)S(1)} %get-tuple-element.7.proj_ref, f32[2048,128]{1,0:T(8,128)S(1)} %get-tuple-element.8.gates_ref, f32[16,128]{1,0:T(8,128)S(1)} %bitcast.39, f32[4,384]{1,0:T(4,128)S(1)} %bitcast_convert_fusion.convw_ref, f32[1]{0:T(128)S(6)} %copy.38.rate_ref, ...), custom_call_target="tpu_custom_call" | custom-call | tf_op jit(solution)/shard_map/delta_mixer/pallas_call | solution.py:131
  185.3 1.0 copy.28
  186.3 16.7 %all-to-all-start = ((bf16[16,128,128]{1,2,0:T(8,128)(2,1)}), bf16[16,128,128]{1,2,0:T(8,128)(2,1)S(1)}, u32[]{:S(2)}, u32[]{:S(2)}) async-start(bf16[16,128,128]{1,2,0:T(8,128)(2,1)} %copy.28), calls=%async_computation | async-start | bytes 1048576 | tf_op jit(solution)/shard_map/all_to_all | solution.py:526
  203.0 0.7 convert_element_type.57
  203.7 0.7 copy.35
  204.4 0.1 copy.30
  204.6 16.3 %all-to-all-done = bf16[16,128,128]{1,2,0:T(8,128)(2,1)S(1)} async-done(((bf16[16,128,128]{1,2,0:T(8,128)(2,1)}), bf16[16,128,128]{1,2,0:T(8,128)(2,1)S(1)}, u32[]{:S(2)}, u32[]{:S(2)}) %all-to-all-start) | async-done | bytes 524320 | tf_op jit(solution)/shard_map/all_to_all | solution.py:526
  220.9 0.0 all-gather.4.cloned.1.call-done
  220.9 0.0 copy-done.2
  220.9 4.7 %multiply_reduce_fusion = (f32[128]{0:T(128)S(1)}, f32[128,2048]{1,0:T(8,128)S(1)}) fusion(bf16[128,2048]{0,1:T(8,128)(2,1)S(1)} %bitcast.42, bf16[1,2048,2048]{2,1,0:T(8,128)(2,1)} %all-gather.4.cloned.1.call-done, bf16[1,128,2048]{2,1,0:T(8,128)(2,1)S(1)} %copy-done.2), kind=kOutput, calls=%fused_computation.6 | convolution fusion | flops 1074790272 | bytes 10486272 | tf_op jit(solution)/shard_map/dot_general | solution.py:528
  225.6 0.0 copy-start.4
  225.6 0.2 multiply_convert_fusion
  225.8 0.0 copy-done
  225.8 0.4 fusion.11
  226.2 0.1 subtract_convert_fusion
  226.3 0.3 concatenate.7.sent_ref
  226.6 0.0 copy-done.4
  226.6 102.3 %expert_exchange.1 = bf16[128,2048]{1,0:T(8,128)(2,1)S(1)} custom-call(bf16[128,2176]{1,0:T(8,128)(2,1)S(1)} %concatenate.7.sent_ref, f32[128,2048]{1,0:T(8,128)} %copy-done.4, bf16[2048,1024]{1,0:T(8,128)(2,1)} %bitcast.41, bf16[512,2048]{1,0:T(8,128)(2,1)} %bitcast.43), custom_call_target="tpu_custom_call" | custom-call | tf_op jit(solution)/shard_map/expert_exchange/pallas_call | solution.py:495
  328.9 0.8 copy.39
  (4 shorter events, 0.0 us)
Async XLA Ops:
  6.5 219.3 %copy-start = (bf16[2048,16]{0,1:T(8,128)(2,1)S(1)}, bf16[2048,16]{0,1:T(8,128)(2,1)}, u32[]{:S(2)}) copy-start(bf16[2048,16]{0,1:T(8,128)(2,1)} %param.27) | copy-start | bytes 196612
  6.5 214.3 %copy-start.2 = (bf16[1,128,2048]{2,1,0:T(8,128)(2,1)S(1)}, bf16[1,128,2048]{2,1,0:T(8,128)(2,1)}, u32[]{:S(2)}) copy-start(bf16[1,128,2048]{2,1,0:T(8,128)(2,1)} %param.15) | copy-start | bytes 1572868
  6.5 214.3 %all-gather.4.cloned.1.call-start = ((), (), s32[]{:S(2)}) async-start(), calls=%async_computation.1 | async-start | bytes 8912896 | tf_op jit(solution)/shard_map/all_gather | solution.py:523
  49.3 1.0 copy-start.1
  133.7 0.7 copy-start.3
  186.3 34.5 %all-to-all-start = ((bf16[16,128,128]{1,2,0:T(8,128)(2,1)}), bf16[16,128,128]{1,2,0:T(8,128)(2,1)S(1)}, u32[]{:S(2)}, u32[]{:S(2)}) async-start(bf16[16,128,128]{1,2,0:T(8,128)(2,1)} %copy.28), calls=%async_computation | async-start | bytes 1048576 | tf_op jit(solution)/shard_map/all_to_all | solution.py:526
  225.6 1.0 copy-start.4
Sparse Core Ops, SparseCore 0:
  44.9 132.9 all-gather.3

commit v3 on v2

v3 whole, which is shorter than its diff:
```python
import functools

import jax
import jax.numpy as jnp
from jax import lax
from jax.experimental import pallas as pl
from jax.experimental.pallas import tpu as pltpu
from jax.sharding import PartitionSpec as P

HD = 128
C = 128
EXPERTS = 16
PASSES = 3
MESH = pl.DeviceIdType.MESH
f32 = jnp.float32
bf16 = jnp.bfloat16
NN = ((1,), (0,))
NT = ((1,), (1,))
TN = ((0,), (0,))


def split(a):
    hi = a.astype(bf16)
    return hi, (a - hi.astype(f32)).astype(bf16)


def dg(a, b, dims=NN):
    return lax.dot_general(a, b, (dims, ((), ())), preferred_element_type=f32)


def mm(a, b, dims=NN, passes=PASSES):
    if passes == 1:
        return dg(a.astype(bf16), b.astype(bf16), dims)
    ah, al = split(a)
    bh, bl = split(b)
    return dg(ah, bh, dims) + (dg(al, bh, dims) + dg(ah, bl, dims))


def chunk_maps(c, gate_ref, docs_ref, win_ref, docc_ref, convw, rate):
    r0 = pl.multiple_of(c * C, C)
    docw = docc_ref[pl.ds(r0, C + 8), :]
    doc_col = docw[8:, :]
    parts = []
    for g in range(3):
        w = win_ref[pl.ds(r0, C + 8), g * HD:(g + 1) * HD]
        acc = w[8:, :] * convw[0:1, g * HD:(g + 1) * HD]
        for j in range(1, 4):
            keep = docw[8 - j:C + 8 - j, :] == doc_col
            acc = acc + jnp.where(keep, w[8 - j:C + 8 - j, :] * convw[j:j + 1, g * HD:(g + 1) * HD], 0.0)
        parts.append(acc * jax.nn.sigmoid(acc))
    q, k, v = parts
    q = q * (lax.rsqrt(jnp.sum(q * q, axis=1, keepdims=True) + 1e-6) * HD ** -0.5)
    k = k * lax.rsqrt(jnp.sum(k * k, axis=1, keepdims=True) + 1e-6)
    gates = gate_ref[pl.ds(r0, C), :]
    beta = jnp.broadcast_to(jax.nn.sigmoid(gates[:, 0:1]), (C, HD))
    d = gates[:, 1:2]
    sp = jnp.maximum(d, 0.0) + jnp.log1p(jnp.exp(-jnp.abs(d)))
    lg = jnp.broadcast_to(-rate * sp, (C, HD))
    row = lax.broadcasted_iota(jnp.int32, (C, C), 0)
    col = lax.broadcasted_iota(jnp.int32, (C, C), 1)
    low = (row >= col)
    tri = low.astype(bf16)
    h0 = lg.astype(bf16)
    r1 = lg - h0.astype(f32)
    h1 = r1.astype(bf16)
    h2 = (r1 - h1.astype(f32)).astype(bf16)
    cum = dg(tri, h0) + (dg(tri, h1) + dg(tri, h2))
    doc_row = docs_ref[pl.ds(c, 1), :]
    keep = jnp.logical_and(low, doc_col == doc_row)
    gap = cum - cum.T
    decay = jnp.where(keep, jnp.exp(jnp.where(keep, gap, 0.0)), 0.0)
    start = jnp.where(doc_col == docw[7:8, :], jnp.exp(cum), 0.0)
    kk = mm(k, k, NT)
    qk = mm(q, k, NT) * decay
    L = jnp.where(row > col, beta * kk * decay, 0.0)
    eye = (row == col).astype(f32)
    T = eye - jnp.where((row >> 1) == (col >> 1), L, 0.0)
    for sh in range(1, 7):
        m = jnp.logical_and((row >> (sh + 1)) == (col >> (sh + 1)), (row >> sh) != (col >> sh))
        T = T - mm(T, mm(jnp.where(m, L, 0.0), T))
    UW = mm(T, jnp.concatenate([beta * v, beta * start * k], axis=1))
    kend = k * decay.T[:, C - 1:C]
    PUW = mm(qk, UW)
    KUW = mm(kend, UW, TN)
    M = eye * start[C - 1:C, :] - KUW[:, HD:]
    Qp = start * q - PUW[:, HD:]
    return Qp, M, PUW[:, :HD], KUW[:, :HD]


def rms_scale(values, gain):
    mean_square = jnp.mean(values * values, axis=-1, keepdims=True)
    return values * lax.rsqrt(mean_square + 1e-06) * gain.astype(f32)


class Place:
    def __init__(self):
        e = lax.axis_index("expert")
        self.e = e
        self.z, self.x, self.c = e // 8, (e // 2) % 4, e % 2

    def at(self, zz, dx, cc=0):
        return ((self.z + zz) % 2 * 4 + (self.x + dx) % 4) * 2 + (self.c + cc) % 2

    def pair(self, zz, dx):
        return ((self.z + zz) % 2 * 4 + (self.x + dx) % 4) * 2


class Copies:
    def __init__(self, send, recv, base):
        self.send, self.recv, self.base, self.sent = send, recv, base, []

    def make(self, i, src, dst, peer):
        return pltpu.make_async_remote_copy(
            src_ref=src, dst_ref=dst, send_sem=self.send.at[self.base + i],
            recv_sem=self.recv.at[self.base + i], device_id=peer, device_id_type=MESH)

    def go(self, i, parts):
        self.make(i, *parts()).start()
        self.sent.append((i, parts))

    def arrive(self, i, dst, peer):
        self.make(i, dst, dst, peer).wait_recv()

    def finish(self):
        for i, parts in self.sent:
            self.make(i, *parts()).wait_send()


GATHER_COPIES = 30


class Gather:
    def __init__(self, full, copies, place, width):
        self.full, self.copies, self.place, self.width = full, copies, place, width
        self.half = full.shape[1] // 2

    def ref(self, zz, dx, h, cc=0):
        return self.full.at[self.place.at(zz, dx, cc), pl.ds(h * self.half, self.half), pl.ds(0, self.width)]

    def peer(self, *r):
        return {"expert": self.place.at(*r)}

    def go(self, n, zz, dx, h, to):
        def parts():
            block = self.ref(zz, dx, h)
            return block, block, self.peer(*to)
        self.copies.go(n, parts)

    def swap(self, zz, dx, h):
        self.go(14 + (zz * 4 + dx) * 2 + h, zz, dx, h, (0, 0, 1))

    def take(self, n, zz, dx, h):
        self.copies.arrive(n, self.ref(zz, dx, h), self.peer(0, 1))
        self.swap(zz, dx, h)

    def swapped(self, zz, dx):
        for h in range(2):
            self.copies.arrive(14 + (zz * 4 + dx) * 2 + h, self.ref(zz, dx, h, 1), self.peer(0, 0, 1))

    def plus(self, zz, h):
        self.go(2 + zz * 2 + h, zz, 0, h, (0, 1))

    def minus(self, zz, h):
        self.go(6 + zz * 2 + h, zz, 0, h, (0, 3))

    def begin(self):
        for h in range(2):
            self.go(h, 0, 0, h, (1, 0))
            self.plus(0, h)
            self.minus(0, 1 - h)
        self.swap(0, 0, 0)
        self.swap(0, 0, 1)

    def from_x(self, zz):
        self.take(2 + zz * 2, zz, 3, 0)
        self.go(10 + zz, zz, 3, 0, (0, 1))
        self.take(6 + zz * 2 + 1, zz, 1, 1)
        self.go(12 + zz, zz, 1, 1, (0, 3))
        self.take(2 + zz * 2 + 1, zz, 3, 1)
        self.take(6 + zz * 2, zz, 1, 0)

    def from_z(self, h):
        self.take(h, 1, 0, h)
        self.plus(1, h)
        self.minus(1, h)

    def from_far(self, zz):
        self.take(10 + zz, zz, 2, 0)
        self.take(12 + zz, zz, 2, 1)


def add_rows(dst, sources, first, count):
    def step(i, _):
        at = pl.ds(pl.multiple_of(first + i * 16, 16), 16)
        total = dst[at, :].astype(f32)
        for source in sources:
            total = total + source[at, :].astype(f32)
        dst[at, :] = total.astype(bf16)
        return 0
    lax.fori_loop(0, count // 16, step, 0)


SEM_TOKENS, SEM_SHARDS, SEM_OUT = 0, GATHER_COPIES, GATHER_COPIES + 19
SEM_HEADS = SEM_OUT + GATHER_COPIES
SEM_ROUTED = SEM_HEADS + 16
SEM_SUMS = SEM_ROUTED + GATHER_COPIES
SEM_ALL = SEM_SUMS + 22


def layer_kernel(tok_ref, docs_ref, ids_ref, gain_ref, pack_ref, conv_ref, rate_ref, hgain_ref, mgain_ref,
                 router_ref, ein_ref, eout_ref, out_ref,
                 full, w, win, branch, gate_ref, docc, maps, adds, obuf, heads, mid, y, kin, ap, am, bp, bm, zb,
                 up, down, hid, send, recv, load):
    place = Place()
    fsdp = lax.axis_index("fsdp")
    fy, fz = fsdp // 4, fsdp % 4
    tok, width = tok_ref.shape
    half = tok // 2
    rows = pack_ref.shape[0]
    ff = down.shape[0]
    chunks = 16 * tok // C

    def line(dy, d):
        return (fy + dy) % 4 * 4 + (fz + d) % 4

    barrier = pltpu.get_barrier_semaphore()
    peers = [{"expert": (place.e + i) % 16} for i in range(1, 16)]
    peers += [{"fsdp": line(*r)} for r in ((1, 0), (3, 0), (0, 1), (0, 2), (0, 3))]
    for peer in peers:
        pl.semaphore_signal(barrier, inc=1, device_id=peer, device_id_type=MESH)
    loads = [pltpu.make_async_copy(ein_ref, up, load.at[0]), pltpu.make_async_copy(eout_ref, down, load.at[1])]
    for copy in loads:
        copy.start()
    w[fsdp] = pack_ref[...]
    full[place.e, :, :width] = rms_scale(tok_ref[...].astype(f32), gain_ref[...]).astype(bf16)
    pl.semaphore_wait(barrier, len(peers))

    tokens = Copies(send, recv, SEM_TOKENS)
    shards = Copies(send, recv, SEM_SHARDS)
    gather = Gather(full, tokens, place, width)

    def shard(dy, d, h=None):
        slot = w.at[line(dy, (4 - d) % 4)]
        return slot if h is None else slot.at[pl.ds(h * (rows // 2), rows // 2)]

    def send_shard(n, at, to):
        def parts():
            ref = shard(*at)
            return ref, ref, {"fsdp": line(*to)}
        shards.go(n, parts)

    def both(d):
        send_shard(3 + d, (0, d), (1, 0))
        send_shard(7 + d, (0, d), (3, 0))

    def along_z(d):
        shards.arrive(d - 1, shard(0, d), {"fsdp": line(0, d)})
        both(d)

    def along_y(d):
        shards.arrive(3 + d, shard(3, d), {"fsdp": line(3, 0)})
        send_shard(11 + d, (3, d, 0), (1, 0))
        shards.arrive(7 + d, shard(1, d), {"fsdp": line(1, 0)})
        send_shard(15 + d, (1, d, 1), (3, 0))

    def far_y(d):
        shards.arrive(11 + d, shard(2, d, 0), {"fsdp": line(3, 0)})
        shards.arrive(15 + d, shard(2, d, 1), {"fsdp": line(1, 0)})

    for d in range(1, 4):
        send_shard(d - 1, (0, 0), (0, d))
    both(0)
    gather.begin()
    win[0:8, :] = jnp.zeros((8, 3 * HD), f32)
    docc[0:8, :] = jnp.full((8, HD), -1.0, f32)

    def spread(c, _):
        at = pl.ds(pl.multiple_of(c * C + 8, 8), C)
        docc[at, :] = jnp.broadcast_to(docs_ref[pl.ds(c, 1), :], (C, C)).T
        return 0
    lax.fori_loop(0, chunks, spread, 0)
    for d in range(1, 4):
        along_z(d)
    gather.from_x(0)
    along_y(0)
    gather.from_z(0)
    along_y(1)
    gather.from_z(1)
    along_y(2)
    gather.from_far(0)
    along_y(3)
    for d in range(4):
        far_y(d)
    for f in range(16):
        y[place.e, :, f * HD:(f + 1) * HD] = w[f, :, 5 * HD:]

    def project(zz):
        for dx in range(4):
            gather.swapped(zz, dx)

        def one(dx, _):
            slot = place.pair(zz, dx)
            x = full[pl.ds(slot, 2), :, :width].reshape(2 * tok, width)
            at = pl.ds(pl.multiple_of(slot * tok, 2 * tok), 2 * tok)
            after = pl.ds(pl.multiple_of(slot * tok + 8, 8), 2 * tok)
            r = dg(x, w[:, :, 0:2 * HD].reshape(16 * rows, 2 * HD)).astype(bf16)
            win[after, 0:2 * HD] = r.astype(f32)
            r = dg(x, w[:, :, 2 * HD:4 * HD].reshape(16 * rows, 2 * HD)).astype(bf16)
            win[after, 2 * HD:] = r[:, :HD].astype(f32)
            branch[at, :] = r[:, HD:]
            gate_ref[at, :] = dg(x, w[:, :, 4 * HD:5 * HD].reshape(16 * rows, HD))
            return 0
        lax.fori_loop(0, 4, one, 0)

    project(0)
    convw = conv_ref[...].astype(f32)
    rate = rate_ref[0]
    outs = Copies(send, recv, SEM_OUT)
    spreads = Gather(y, outs, place, width)

    def other_half():
        project(1)
        spreads.begin()

    events = {
        1: lambda: gather.from_x(1),
        2: lambda: gather.from_far(1),
        3: other_half,
        4: lambda: spreads.from_x(0),
        5: lambda: spreads.from_far(0),
        6: lambda: spreads.from_z(0),
        7: lambda: spreads.from_z(1),
    }

    def two_chunks(i, _):
        for step, event in events.items():
            pl.when(i == step)(event)
        first = (i + 5 * place.z) % 8 * 2
        for c in (first, first + 1):
            q_map, s_map, q_add, s_add = chunk_maps(c, gate_ref, docs_ref, win, docc, convw, rate)
            maps[c, :C, :] = q_map
            maps[c, C:, :] = s_map
            adds[c, :C, :] = q_add
            adds[c, C:, :] = s_add
        return 0
    lax.fori_loop(0, chunks // 2, two_chunks, 0)
    tokens.finish()
    spreads.from_x(1)

    def head_copy(c):
        return pltpu.make_async_remote_copy(
            src_ref=obuf.at[c], dst_ref=heads.at[:, pl.ds(pl.multiple_of(place.e * HD, HD), HD)],
            send_sem=send.at[SEM_HEADS + c], recv_sem=recv.at[SEM_HEADS + place.e],
            device_id={"expert": c}, device_id_type=MESH)

    hgain = hgain_ref[...].astype(f32)

    def advance(c, S):
        r0 = pl.multiple_of(c * C, C)
        two = mm(maps[c], S) + adds[c]
        o = two[:C, :]
        g = branch[pl.ds(r0, C), :].astype(f32)
        obuf[c] = (rms_scale(o, hgain) * (g * jax.nn.sigmoid(g))).astype(bf16)

        @pl.when(c != place.e)
        def _():
            head_copy(c).start()
        return two[C:, :]
    S = lax.fori_loop(0, chunks // 2, advance, jnp.zeros((HD, HD), f32))
    spreads.from_far(1)
    lax.fori_loop(chunks // 2, chunks, advance, S)
    for zz in range(2):
        for dx in range(4):
            spreads.swapped(zz, dx)
    heads[:, pl.ds(pl.multiple_of(place.e * HD, HD), HD)] = obuf[place.e]

    def head_in(h, _):
        @pl.when(h != place.e)
        def _():
            pltpu.make_async_remote_copy(
                src_ref=obuf.at[h], dst_ref=heads.at[:, pl.ds(pl.multiple_of(h * HD, HD), HD)],
                send_sem=send.at[SEM_HEADS + h], recv_sem=recv.at[SEM_HEADS + h],
                device_id={"expert": h}, device_id_type=MESH).wait_recv()
        return 0
    lax.fori_loop(0, 16, head_in, 0)
    nf, nd = min(256, ff), min(256, width)

    def out_project(j, _):
        cols = pl.ds(pl.multiple_of(j * nd, nd), nd)
        mid[:, cols] = tok_ref[:, cols].astype(f32) + dg(heads[...], y[:, :, cols].reshape(16 * HD, nd))
        return 0
    lax.fori_loop(0, width // nd, out_project, 0)
    moe_in = rms_scale(mid[...], mgain_ref[...]).astype(bf16)
    full[place.e, :, :width] = moe_in
    logits = dg(full[place.e, :, :width], router_ref[...])
    lane = lax.broadcasted_iota(jnp.int32, (tok, HD), 1)
    ids = ids_ref[...]
    picked = lane < 0
    for k in range(ids.shape[1]):
        picked = jnp.logical_or(picked, ids[:, k:k + 1] == lane % EXPERTS)
    raised = jnp.where(picked, jnp.exp(logits), 0.0)
    weights = raised / jnp.sum(jnp.where(lane < EXPERTS, raised, 0.0), axis=1, keepdims=True)
    upper = weights.astype(bf16).astype(f32)
    side = jnp.where(lane < EXPERTS, upper, jnp.where(lane < 2 * EXPERTS, weights - upper, 0.0))
    full[place.e, :, width:] = side.astype(bf16)
    outs.finish()

    routed = Copies(send, recv, SEM_ROUTED)
    sums = Copies(send, recv, SEM_SUMS)
    gather = Gather(full, routed, place, width + HD)
    gather.begin()
    for copy in loads:
        copy.wait()
    plus, minus = (lambda: {"expert": place.at(0, 1)}), (lambda: {"expert": place.at(0, 3)})
    over, twin = (lambda: {"expert": place.at(1, 0)}), (lambda: {"expert": place.at(0, 0, 1)})

    def compute(zz, dx):
        gather.swapped(zz, dx)
        pair = pl.ds(place.pair(zz, dx), 2)
        at = lax.broadcasted_iota(jnp.int32, (2 * tok, HD), 1)
        values = full[pair, :, width:].reshape(2 * tok, HD).astype(f32)
        hit = jnp.logical_or(at == place.e, at == place.e + EXPERTS)
        weight = jnp.sum(jnp.where(hit, values, 0.0), axis=1, keepdims=True)

        def inner(j, _):
            x = full[pair, :, :width].reshape(2 * tok, width)
            g = dg(x, up[:, pl.ds(pl.multiple_of(j * nf, nf), nf)])
            u = dg(x, up[:, pl.ds(pl.multiple_of(ff + j * nf, nf), nf)])
            hid[:, pl.ds(pl.multiple_of(j * nf, nf), nf)] = (g * jax.nn.sigmoid(g) * u).astype(bf16)
            return 0
        lax.fori_loop(0, ff // nf, inner, 0)

        def outer(j, _):
            cols = pl.ds(pl.multiple_of(j * nd, nd), nd)
            out = dg(hid[...], down[:, cols]) * weight
            y[pair, :, cols] = out.astype(bf16).reshape(2, tok, nd)
            return 0
        lax.fori_loop(0, width // nd, outer, 0)
        sums.go(zz * 4 + dx, lambda: (y.at[place.at(zz, dx, 1)], kin.at[zz * 4 + dx], twin()))

    def own(zz, dx):
        return y.at[place.at(zz, dx)]

    def chip_sum(zz, dx):
        sums.arrive(zz * 4 + dx, kin.at[zz * 4 + dx], twin())
        add_rows(own(zz, dx), [kin.at[zz * 4 + dx]], 0, tok)

    low, high = pl.ds(0, half), pl.ds(half, half)

    def far(zz):
        chip_sum(zz, 2)
        sums.go(8 + zz, lambda: (own(zz, 2).at[low], ap.at[zz], plus()))
        sums.go(10 + zz, lambda: (own(zz, 2).at[high], am.at[zz], minus()))

    def near(zz):
        chip_sum(zz, 1)
        sums.go(12 + zz, lambda: (own(zz, 1).at[high], bp.at[zz, high], plus()))
        chip_sum(zz, 3)
        sums.go(14 + zz, lambda: (own(zz, 3).at[low], bm.at[zz, low], minus()))

    def relay(zz):
        sums.arrive(8 + zz, ap.at[zz], minus())
        add_rows(own(zz, 1).at[low], [ap.at[zz]], 0, half)
        sums.go(16 + zz, lambda: (own(zz, 1).at[low], bp.at[zz, low], plus()))
        sums.arrive(10 + zz, am.at[zz], plus())
        add_rows(own(zz, 3).at[high], [am.at[zz]], 0, half)
        sums.go(18 + zz, lambda: (own(zz, 3).at[high], bm.at[zz, high], minus()))

    def settle(zz, h):
        if h == 0:
            sums.arrive(14 + zz, bm.at[zz, low], plus())
            sums.arrive(16 + zz, bp.at[zz, low], minus())
        else:
            sums.arrive(12 + zz, bp.at[zz, high], minus())
            sums.arrive(18 + zz, bm.at[zz, high], plus())

    compute(0, 0)
    gather.from_x(0)
    compute(0, 3)
    gather.from_z(0)
    compute(0, 1)
    gather.from_z(1)
    gather.from_far(0)
    compute(0, 2)
    gather.from_x(1)
    far(0)
    compute(1, 0)
    near(0)
    gather.from_far(1)
    compute(1, 3)
    relay(0)
    compute(1, 1)
    compute(1, 2)
    far(1)
    near(1)
    relay(1)
    chip_sum(1, 0)
    for h, part in ((0, low), (1, high)):
        settle(1, h)
        add_rows(own(1, 0), [bp.at[1], bm.at[1]], h * half, half)
        sums.go(20 + h, lambda part=part: (own(1, 0).at[part], zb.at[part], over()))
    chip_sum(0, 0)
    for h, part in ((0, low), (1, high)):
        settle(0, h)
        sums.arrive(20 + h, zb.at[part], over())

        def last(i, _):
            at = pl.ds(pl.multiple_of(h * half + i * 16, 16), 16)
            total = mid[at, :]
            for source in (own(0, 0), bp.at[0], bm.at[0], zb):
                total = total + source[at, :].astype(f32)
            out_ref[at, :] = total.astype(bf16)
            return 0
        lax.fori_loop(0, half // 16, last, 0)

    def head_out(c, _):
        @pl.when(c != place.e)
        def _():
            head_copy(c).wait_send()
        return 0
    lax.fori_loop(0, chunks, head_out, 0)
    shards.finish()
    routed.finish()
    sums.finish()


def layer_call(tokens, docs, ids, gain, packed, conv, rate, hgain, mgain, router, expert_in, expert_out):
    tok, width = tokens.shape
    rows, cols = packed.shape
    ff = expert_out.shape[0]
    seq = 16 * tok
    V, A = pl.BlockSpec(memory_space=pltpu.VMEM), pl.BlockSpec(memory_space=pl.ANY)
    S = pl.BlockSpec(memory_space=pltpu.SMEM)

    def vm(*s):
        return pltpu.VMEM(s, bf16)

    def vf(*s):
        return pltpu.VMEM(s, f32)
    sem = pltpu.SemaphoreType.DMA
    return pl.pallas_call(
        layer_kernel,
        out_shape=jax.ShapeDtypeStruct((tok, width), bf16),
        in_specs=[V, V, V, V, V, V, S, V, V, V, A, A],
        out_specs=V,
        scratch_shapes=[
            vm(16, tok, width + HD), vm(16, rows, cols), vf(seq + 8, 3 * HD), vm(seq, HD), vf(seq, HD),
            vf(seq + 8, HD), vf(seq // C, 2 * C, HD), vf(seq // C, 2 * C, HD), vm(seq // C, C, HD),
            vm(tok, 16 * HD), vf(tok, width), vm(16, tok, width), vm(8, tok, width),
            vm(2, tok // 2, width), vm(2, tok // 2, width), vm(2, tok, width), vm(2, tok, width), vm(tok, width),
            vm(width, 2 * ff), vm(ff, width), vm(2 * tok, ff), sem((SEM_ALL,)), sem((SEM_ALL,)), sem((2,))],
        compiler_params=pltpu.CompilerParams(collective_id=0, has_side_effects=True,
                                             vmem_limit_bytes=60 * 1024 * 1024),
        name="whole_layer",
    )(tokens, docs, ids, gain, packed, conv, rate, hgain, mgain, router, expert_in, expert_out)


def on_device(tokens, doc_ids, route_ids, norm_gain, proj_weight, gating_weight, block_scale,
              conv_weight, decay_rate, head_gain, out_weight, moe_gain, router_weight,
              expert_in, expert_out):
    scale = jnp.repeat(block_scale[0, 0].astype(f32), HD)
    scaled = (proj_weight[:, 0, :].astype(f32) * scale[None, :]).astype(bf16)
    packed = jnp.concatenate(
        [scaled, jnp.pad(gating_weight[:, :, 0], ((0, 0), (0, HD - 2))), out_weight[0]], 1)
    router = jnp.pad(jnp.concatenate([router_weight, router_weight], 1), ((0, 0), (0, HD - 2 * EXPERTS)))
    return layer_call(
        tokens[0], doc_ids[0].astype(f32).reshape(-1, C), route_ids[0], norm_gain.reshape(1, -1), packed,
        conv_weight[0], decay_rate, head_gain.reshape(1, -1), moe_gain.reshape(1, -1), router,
        expert_in[0], expert_out[0])[None]


def solution(mesh):
    placed = (
        P("fsdp", "expert", None),
        P("fsdp", None),
        P("fsdp", "expert", None),
        P(),
        P("fsdp", "expert", None),
        P("fsdp", None, "expert"),
        P("fsdp", "expert", None),
        P("expert", None, None),
        P("expert"),
        P(),
        P("expert", None, "fsdp"),
        P(),
        P(),
        P("expert", None, None),
        P("expert", None, None),
    )
    return jax.shard_map(
        on_device, mesh=mesh, in_specs=placed, out_specs=P("fsdp", "expert", None), check_vma=False
    )
```

time: 337 us -> 279 us (0.83)
  blocking collectives: 38.2 us -> 0 us
  Pallas kernels: 236 us -> 265 us
  starting transfers between devices: 16.7 us -> 0 us
  waiting for transfers between devices: 16.3 us -> 0 us
  between operations: 14.2 us -> 0.68 us
  matrix products: 5.1 us -> 0 us
    all_gather x1 -> x0, blocking collectives: 38.2 us -> none  [on_device(): lax.all_gather(out_weight[0], 'fsdp', axis=1, tiled=True)]
    pallas_call x3 -> x1, Pallas kernels: 236 us -> 265 us  [layer_call(): pl.pallas_call(layer_kernel, out_shape=jax.ShapeDtypeStruct((tok, width),...]
    all_to_all x1 -> x0, starting transfers between devices: 16.7 us -> none  [on_device(): lax.all_to_all(head_out.reshape(-1, tok, HD), 'expert', split_axis=0, con...]
    all_to_all x1 -> x0, waiting for transfers between devices: 16.3 us -> none  [on_device(): lax.all_to_all(head_out.reshape(-1, tok, HD), 'expert', split_axis=0, con...]
    dot_general x2 -> x0, matrix products: 5.1 us -> none  [the longest x1 4.74 us: on_device(): mid = residual + jnp.dot(mine, out_full, preferred_element_type=f32)]
  transfers between devices with their start and end apart: 2 -> 0, of which waited for: 1 -> 0; matrix products, arithmetic and copies ran while one was open for 2% -> 0% of each run, Pallas kernels for 40% -> 0%
where the time goes in v3:
time: 279 us
  Pallas kernels  265 us (95%)
  local copies, waits for them, and re-layouts  7.9 us (3%)
  other arithmetic  5.25 us (2%)
    pallas_call x1, Pallas kernels, layer_call(): pl.pallas_call(layer_kernel, out_shape=jax.ShapeDtypeStruct((tok, width),...  265 us

profile of v3, /device:TPU:39, one launch (start us, length us, event | category | flops | bytes accessed | tf_op | source)
XLA Modules:
  0.0 278.7 jit_solution(15620266694950719078)
XLA Ops:
  0.7 0.7 bitcast_convert_fusion
  1.3 0.1 broadcast_bitcast_fusion
  1.4 1.3 convert_element_type.26
  2.7 1.3 reshape.17.gain_ref
  4.0 1.3 reshape.19.mgain_ref
  5.2 0.8 copy.21
  6.0 1.4 copy.20
  7.4 0.9 fusion.2
  8.4 1.5 fusion.4.pack_ref
  9.8 0.9 pad_maximum_fusion
  10.8 0.3 copy.22
  11.0 0.9 pad.9.router_ref
  11.9 264.9 %whole_layer.1 = bf16[128,2048]{1,0:T(8,128)(2,1)} custom-call(bf16[128,2048]{1,0:T(8,128)(2,1)} %bitcast.21, f32[16,128]{1,0:T(8,128)} %bitcast.25, s32[128,10]{1,0:T(8,128)} %bitcast.22, bf16[1,2048]{1,0:T(2,128)(2,1)} %reshape.17.gain_ref, bf16[128,768]{1,0:T(8,128)(2,1)} %fusion.4.pack_ref, bf16[4,384]{1,0:T(4,128)(2,1)} %bitcast.26, ...), custom_call_target="tpu_custom_call" | custom-call | tf_op jit(solution)/shard_map/whole_layer/pallas_call | solution.py:541
  276.9 1.9 copy.25

commit v4 on v3

v4 whole, which is shorter than its diff:
```python
import functools

import jax
import jax.numpy as jnp
from jax import lax
from jax.experimental import pallas as pl
from jax.experimental.pallas import tpu as pltpu
from jax.sharding import PartitionSpec as P

HD = 128
C = 128
EXPERTS = 16
PASSES = 3
MESH = pl.DeviceIdType.MESH
f32 = jnp.float32
bf16 = jnp.bfloat16
NN = ((1,), (0,))
NT = ((1,), (1,))
TN = ((0,), (0,))


def split(a):
    hi = a.astype(bf16)
    return hi, (a - hi.astype(f32)).astype(bf16)


def dg(a, b, dims=NN):
    return lax.dot_general(a, b, (dims, ((), ())), preferred_element_type=f32)


def mm(a, b, dims=NN, passes=PASSES):
    if passes == 1:
        return dg(a.astype(bf16), b.astype(bf16), dims)
    ah, al = split(a)
    bh, bl = split(b)
    return dg(ah, bh, dims) + (dg(al, bh, dims) + dg(ah, bl, dims))


def chunk_maps(c, gate_ref, docs_ref, win_ref, docc_ref, convw, rate):
    r0 = pl.multiple_of(c * C, C)
    docw = docc_ref[pl.ds(r0, C + 8), :]
    doc_col = docw[8:, :]
    parts = []
    for g in range(3):
        w = win_ref[pl.ds(r0, C + 8), g * HD:(g + 1) * HD]
        acc = w[8:, :] * convw[0:1, g * HD:(g + 1) * HD]
        for j in range(1, 4):
            keep = docw[8 - j:C + 8 - j, :] == doc_col
            acc = acc + jnp.where(keep, w[8 - j:C + 8 - j, :] * convw[j:j + 1, g * HD:(g + 1) * HD], 0.0)
        parts.append(acc * jax.nn.sigmoid(acc))
    q, k, v = parts
    q = q * (lax.rsqrt(jnp.sum(q * q, axis=1, keepdims=True) + 1e-6) * HD ** -0.5)
    k = k * lax.rsqrt(jnp.sum(k * k, axis=1, keepdims=True) + 1e-6)
    gates = gate_ref[pl.ds(r0, C), :]
    beta = jnp.broadcast_to(jax.nn.sigmoid(gates[:, 0:1]), (C, HD))
    d = gates[:, 1:2]
    sp = jnp.maximum(d, 0.0) + jnp.log1p(jnp.exp(-jnp.abs(d)))
    lg = jnp.broadcast_to(-rate * sp, (C, HD))
    row = lax.broadcasted_iota(jnp.int32, (C, C), 0)
    col = lax.broadcasted_iota(jnp.int32, (C, C), 1)
    low = (row >= col)
    tri = low.astype(bf16)
    h0 = lg.astype(bf16)
    r1 = lg - h0.astype(f32)
    h1 = r1.astype(bf16)
    h2 = (r1 - h1.astype(f32)).astype(bf16)
    cum = dg(tri, h0) + (dg(tri, h1) + dg(tri, h2))
    doc_row = docs_ref[0:1, pl.ds(r0, C)].astype(f32)
    keep = jnp.logical_and(low, doc_col == doc_row)
    gap = cum - cum.T
    decay = jnp.where(keep, jnp.exp(jnp.where(keep, gap, 0.0)), 0.0)
    start = jnp.where(doc_col == docw[7:8, :], jnp.exp(cum), 0.0)
    kk = mm(k, k, NT)
    qk = mm(q, k, NT) * decay
    L = jnp.where(row > col, beta * kk * decay, 0.0)
    eye = (row == col).astype(f32)
    T = eye - jnp.where((row >> 1) == (col >> 1), L, 0.0)
    for sh in range(1, 7):
        m = jnp.logical_and((row >> (sh + 1)) == (col >> (sh + 1)), (row >> sh) != (col >> sh))
        T = T - mm(T, mm(jnp.where(m, L, 0.0), T))
    UW = mm(T, jnp.concatenate([beta * v, beta * start * k], axis=1))
    kend = k * decay.T[:, C - 1:C]
    PUW = mm(qk, UW)
    KUW = mm(kend, UW, TN)
    M = eye * start[C - 1:C, :] - KUW[:, HD:]
    Qp = start * q - PUW[:, HD:]
    return Qp, M, PUW[:, :HD], KUW[:, :HD]


def rms_scale(values, gain):
    mean_square = jnp.mean(values * values, axis=-1, keepdims=True)
    return values * lax.rsqrt(mean_square + 1e-06) * gain.astype(f32)


class Place:
    def __init__(self):
        e = lax.axis_index("expert")
        self.e = e
        self.z, self.x, self.c = e // 8, (e // 2) % 4, e % 2

    def at(self, zz, dx, cc=0):
        return ((self.z + zz) % 2 * 4 + (self.x + dx) % 4) * 2 + (self.c + cc) % 2

    def pair(self, zz, dx):
        return ((self.z + zz) % 2 * 4 + (self.x + dx) % 4) * 2


class Copies:
    def __init__(self, send, recv, base):
        self.send, self.recv, self.base, self.sent = send, recv, base, []

    def make(self, i, src, dst, peer):
        return pltpu.make_async_remote_copy(
            src_ref=src, dst_ref=dst, send_sem=self.send.at[self.base + i],
            recv_sem=self.recv.at[self.base + i], device_id=peer, device_id_type=MESH)

    def go(self, i, parts):
        self.make(i, *parts()).start()
        self.sent.append((i, parts))

    def arrive(self, i, dst, peer):
        self.make(i, dst, dst, peer).wait_recv()

    def finish(self):
        for i, parts in self.sent:
            self.make(i, *parts()).wait_send()


GATHER_COPIES = 36
PIECES = 4
ORDER = ((0, 0), (0, 1), (1, 0), (0, 2), (1, 1), (0, 3), (1, 2), (1, 3))


class Gather:
    def __init__(self, full, copies, place, width):
        self.full, self.copies, self.place, self.width = full, copies, place, width
        self.rows = full.shape[3] // PIECES

    def piece(self, r):
        return pl.ds(r * self.rows, self.rows)

    def ref(self, zz, dx, r):
        p = self.place
        return self.full.at[(p.z + zz) % 2, (p.x + dx) % 4, p.c, self.piece(r), pl.ds(0, self.width)]

    def column(self, zz, r, cc):
        p = self.place
        return self.full.at[(p.z + zz) % 2, :, (p.c + cc) % 2, self.piece(r), pl.ds(0, self.width)]

    def peer(self, *r):
        return {"expert": self.place.at(*r)}

    def go(self, n, zz, dx, r, to):
        def parts():
            block = self.ref(zz, dx, r)
            return block, block, self.peer(*to)
        self.copies.go(n, parts)

    def across(self, r):
        self.go(r, 0, 0, r, (1, 0))

    def out(self, zz, r):
        self.go(4 + zz * 4 + r, zz, 0, r, (0, 1))
        self.go(12 + zz * 4 + r, zz, 0, r, (0, 3))

    def begin(self):
        for r in range(2):
            self.across(r)
            self.out(0, r)

    def near(self, zz, r):
        plus = lambda: self.copies.arrive(4 + zz * 4 + r, self.ref(zz, 3, r), self.peer(0, 1))
        minus = lambda: self.copies.arrive(12 + zz * 4 + r, self.ref(zz, 1, r), self.peer(0, 1))
        if r % 2 == 0:
            plus()
            self.go(20 + zz * 4 + r, zz, 3, r, (0, 1))
            minus()
        else:
            minus()
            self.go(20 + zz * 4 + r, zz, 1, r, (0, 3))
            plus()
        if zz == 0 and r + 2 < PIECES:
            self.out(0, r + 2)

    def crossed(self, r):
        self.copies.arrive(r, self.ref(1, 0, r), self.peer(1, 0))
        self.out(1, r)
        if r + 2 < PIECES:
            self.across(r + 2)

    def advance(self, k):
        zz, r = ORDER[k]
        self.near(zz, r)
        if k + 1 < len(ORDER) and ORDER[k + 1][0] == 1:
            self.crossed(ORDER[k + 1][1])
        self.copies.arrive(20 + zz * 4 + r, self.ref(zz, 2, r), self.peer(0, 1))

        def parts():
            block = self.column(zz, r, 0)
            return block, block, self.peer(0, 0, 1)
        self.copies.go(28 + zz * 4 + r, parts)

    def swapped(self, zz, r):
        self.copies.arrive(28 + zz * 4 + r, self.column(zz, r, 1), self.peer(0, 0, 1))


class Shards:
    def __init__(self, buf, copies, line, cut):
        self.buf, self.copies, self.line, self.cut = buf, copies, line, cut

    def ref(self, dy, d, h=None):
        slot = self.buf.at[self.line(dy, (4 - d) % 4)]
        if h is None:
            return slot
        return slot.at[pl.ds(0, self.cut)] if h == 0 else slot.at[pl.ds(self.cut, self.buf.shape[1] - self.cut)]

    def peer(self, *r):
        return {"fsdp": self.line(*r)}

    def go(self, n, at, to):
        def parts():
            ref = self.ref(*at)
            return ref, ref, self.peer(*to)
        self.copies.go(n, parts)

    def both(self, d):
        self.go(3 + d, (0, d), (1, 0))
        self.go(7 + d, (0, d), (3, 0))

    def begin(self):
        for d in range(1, 4):
            self.go(d - 1, (0, 0), (0, d))
        self.both(0)

    def along_z(self, d):
        self.copies.arrive(d - 1, self.ref(0, d), self.peer(0, d))
        self.both(d)

    def along_y(self, d):
        self.copies.arrive(3 + d, self.ref(3, d), self.peer(3, 0))
        self.go(11 + d, (3, d, 0), (1, 0))
        self.copies.arrive(7 + d, self.ref(1, d), self.peer(1, 0))
        self.go(15 + d, (1, d, 1), (3, 0))

    def far_y(self, d):
        self.copies.arrive(11 + d, self.ref(2, d, 0), self.peer(3, 0))
        self.copies.arrive(15 + d, self.ref(2, d, 1), self.peer(1, 0))


def add_rows(dst, sources, count):
    def step(i, _):
        at = pl.ds(pl.multiple_of(i * 16, 16), 16)
        total = sources[0][at, :].astype(f32)
        for source in sources[1:]:
            total = total + source[at, :].astype(f32)
        dst[at, :] = total.astype(bf16)
        return 0
    lax.fori_loop(0, count // 16, step, 0)


SEM_TOKENS, SEM_SHARDS, SEM_COLS = 0, GATHER_COPIES, GATHER_COPIES + 19
SEM_OUT = SEM_COLS + 19
SEM_HEADS = SEM_OUT + GATHER_COPIES
SEM_ROUTED = SEM_HEADS + 16
SEM_SUMS = SEM_ROUTED + GATHER_COPIES
SEM_ALL = SEM_SUMS + 36


def layer_kernel(tok_ref, docs_ref, ids_ref, gains_ref, pack_ref, cols_ref, conv_ref, rate_ref, hgain_ref,
                 router_ref, ein_ref, eout_ref, out_ref,
                 full, w, gw, oc, win, branch, gate_ref, docc, maps, adds, obuf, heads, mid, y, kin, ap, bp, bm, zb,
                 up, down, hid, send, recv, load):
    place = Place()
    fsdp = lax.axis_index("fsdp")
    fy, fz = fsdp // 4, fsdp % 4
    tok, width = tok_ref.shape
    part = tok // PIECES
    ff = down.shape[0]
    chunks = 16 * tok // C
    rows = width // 16

    def line(dy, d):
        return (fy + dy) % 4 * 4 + (fz + d) % 4

    barrier = pltpu.get_barrier_semaphore()
    peers = [{"expert": (place.e + i) % 16} for i in range(1, 16)]
    peers += [{"fsdp": line(*r)} for r in ((1, 0), (3, 0), (0, 1), (0, 2), (0, 3))]
    for peer in peers:
        pl.semaphore_signal(barrier, inc=1, device_id=peer, device_id_type=MESH)
    loads = [pltpu.make_async_copy(ein_ref, up, load.at[0]), pltpu.make_async_copy(eout_ref, down, load.at[1])]
    for copy in loads:
        copy.start()
    w[fsdp] = pack_ref[...]
    oc[fsdp] = cols_ref[...]
    full[place.z, place.x, place.c, :, :width] = rms_scale(tok_ref[...].astype(f32), gains_ref[0:1, :]).astype(bf16)
    pl.semaphore_wait(barrier, len(peers))

    tokens = Copies(send, recv, SEM_TOKENS)
    weights_in = Copies(send, recv, SEM_SHARDS)
    columns_in = Copies(send, recv, SEM_COLS)
    gather = Gather(full, tokens, place, width)
    shards = Shards(w, weights_in, line, rows // 2)
    columns = Shards(oc, columns_in, line, HD // 2)
    shards.begin()
    gather.begin()
    win[0:8, :] = jnp.zeros((8, 3 * HD), f32)
    docc[0:8, :] = jnp.full((8, HD), -1.0, f32)

    def spread(c, _):
        r0 = pl.multiple_of(c * C, C)
        docs = docs_ref[0:1, pl.ds(r0, C)].astype(f32)
        docc[pl.ds(pl.multiple_of(r0 + 8, 8), C), :] = jnp.broadcast_to(docs, (C, C)).T
        return 0
    lax.fori_loop(0, chunks, spread, 0)
    gather.advance(0)
    for d in range(1, 4):
        shards.along_z(d)
    gather.advance(1)
    for d in range(4):
        shards.along_y(d)
        gather.advance(2 + d)
    for d in range(4):
        shards.far_y(d)
    columns.begin()
    for f in range(16):
        gw[:, f * rows:(f + 1) * rows] = w[f, rows:, :rows]

    def project(zz):
        for r in range(PIECES):
            gather.swapped(zz, r)

        def one(xx, _):
            zi = (place.z + zz) % 2
            slot = zi * 8 + xx * 2
            x = full[zi, xx, :, :, :width].reshape(2 * tok, width)
            at = pl.ds(pl.multiple_of(slot * tok, 2 * tok), 2 * tok)
            after = pl.ds(pl.multiple_of(slot * tok + 8, 8), 2 * tok)
            r = dg(x, w[:, :rows, 0:2 * HD].reshape(16 * rows, 2 * HD)).astype(bf16)
            win[after, 0:2 * HD] = r.astype(f32)
            r = dg(x, w[:, :rows, 2 * HD:4 * HD].reshape(16 * rows, 2 * HD)).astype(bf16)
            win[after, 2 * HD:] = r[:, :HD].astype(f32)
            branch[at, :] = r[:, HD:]
            gate_ref[at, :] = dg(x, gw[...], NT)
            return 0
        lax.fori_loop(0, 4, one, 0)

    project(0)
    convw = conv_ref[...].astype(f32)
    rate = rate_ref[0]
    outs = Copies(send, recv, SEM_OUT)
    spreads = Gather(y, outs, place, width)

    def at_0():
        gather.advance(6)
        for d in range(1, 4):
            columns.along_z(d)

    def at_1():
        gather.advance(7)
        for d in range(4):
            columns.along_y(d)

    def at_2():
        for d in range(4):
            columns.far_y(d)
        for f in range(16):
            y[place.z, place.x, place.c, :, f * HD:(f + 1) * HD] = oc[f]
        spreads.begin()

    def at_3():
        project(1)
        spreads.advance(0)

    def at_4():
        spreads.advance(1)
        spreads.advance(2)

    events = (at_0, at_1, at_2, at_3, at_4, lambda: spreads.advance(3), lambda: spreads.advance(4),
              lambda: spreads.advance(5))

    def two_chunks(i, _):
        for step, event in enumerate(events):
            pl.when(i == step)(event)
        first = (i + 5 * place.z) % 8 * 2
        for c in (first, first + 1):
            q_map, s_map, q_add, s_add = chunk_maps(c, gate_ref, docs_ref, win, docc, convw, rate)
            maps[c, :C, :] = q_map
            maps[c, C:, :] = s_map
            adds[c, :C, :] = q_add
            adds[c, C:, :] = s_add
        return 0
    lax.fori_loop(0, chunks // 2, two_chunks, 0)
    tokens.finish()

    def head_copy(c):
        return pltpu.make_async_remote_copy(
            src_ref=obuf.at[c], dst_ref=heads.at[:, pl.ds(pl.multiple_of(place.e * HD, HD), HD)],
            send_sem=send.at[SEM_HEADS + c], recv_sem=recv.at[SEM_HEADS + place.e],
            device_id={"expert": c}, device_id_type=MESH)

    hgain = hgain_ref[...].astype(f32)

    def advance(c, S):
        r0 = pl.multiple_of(c * C, C)
        two = mm(maps[c], S) + adds[c]
        o = two[:C, :]
        g = branch[pl.ds(r0, C), :].astype(f32)
        obuf[c] = (rms_scale(o, hgain) * (g * jax.nn.sigmoid(g))).astype(bf16)

        @pl.when(c != place.e)
        def _():
            head_copy(c).start()
        return two[C:, :]
    S = lax.fori_loop(0, chunks // 2, advance, jnp.zeros((HD, HD), f32))
    spreads.advance(6)
    lax.fori_loop(chunks // 2, chunks, advance, S)
    spreads.advance(7)
    for zz, r in ORDER:
        spreads.swapped(zz, r)
    heads[:, pl.ds(pl.multiple_of(place.e * HD, HD), HD)] = obuf[place.e]

    def head_in(h, _):
        @pl.when(h != place.e)
        def _():
            pltpu.make_async_remote_copy(
                src_ref=obuf.at[h], dst_ref=heads.at[:, pl.ds(pl.multiple_of(h * HD, HD), HD)],
                send_sem=send.at[SEM_HEADS + h], recv_sem=recv.at[SEM_HEADS + h],
                device_id={"expert": h}, device_id_type=MESH).wait_recv()
        return 0
    lax.fori_loop(0, 16, head_in, 0)
    nf, nd = min(256, ff), min(256, width)

    def out_project(j, _):
        cols = pl.ds(pl.multiple_of(j * nd, nd), nd)
        mid[:, cols] = tok_ref[:, cols].astype(f32) + dg(heads[...], y[:, :, :, :, cols].reshape(16 * HD, nd))
        return 0
    lax.fori_loop(0, width // nd, out_project, 0)
    moe_in = rms_scale(mid[...], gains_ref[1:2, :]).astype(bf16)
    full[place.z, place.x, place.c, :, :width] = moe_in
    logits = dg(moe_in, router_ref[...])
    lane = lax.broadcasted_iota(jnp.int32, (tok, EXPERTS), 1)
    ids = ids_ref[...]
    picked = lane < 0
    for k in range(ids.shape[1]):
        picked = jnp.logical_or(picked, ids[:, k:k + 1] == lane)
    raised = jnp.where(picked, jnp.exp(logits), 0.0)
    weights = raised / jnp.sum(raised, axis=1, keepdims=True)
    upper, lower = split(weights)
    place_row = lax.broadcasted_iota(jnp.int32, (EXPERTS, HD), 0)
    place_col = lax.broadcasted_iota(jnp.int32, (EXPERTS, HD), 1)
    side = dg(upper, (place_col == place_row).astype(bf16)) + dg(lower, (place_col == place_row + EXPERTS).astype(bf16))
    full[place.z, place.x, place.c, :, width:] = side.astype(bf16)
    outs.finish()

    routed = Copies(send, recv, SEM_ROUTED)
    sums = Copies(send, recv, SEM_SUMS)
    gather = Gather(full, routed, place, width + HD)
    gather.begin()
    for copy in loads:
        copy.wait()
    plus, minus = (lambda: {"expert": place.at(0, 1)}), (lambda: {"expert": place.at(0, 3)})
    over, twin = (lambda: {"expert": place.at(1, 0)}), (lambda: {"expert": place.at(0, 0, 1)})

    def rows_of(r):
        return pl.ds(r * part, part)

    def half(zz):
        return (place.z + zz) % 2

    def compute(zz, r):
        gather.swapped(zz, r)
        n = 8 * part
        at = lax.broadcasted_iota(jnp.int32, (n, HD), 1)
        values = full[half(zz), :, :, r * part:(r + 1) * part, width:].reshape(n, HD).astype(f32)
        hit = jnp.logical_or(at == place.e, at == place.e + EXPERTS)
        weight = jnp.sum(jnp.where(hit, values, 0.0), axis=1, keepdims=True)

        def inner(j, _):
            x = full[half(zz), :, :, r * part:(r + 1) * part, :width].reshape(n, width)
            g = dg(x, up[:, pl.ds(pl.multiple_of(j * nf, nf), nf)])
            u = dg(x, up[:, pl.ds(pl.multiple_of(ff + j * nf, nf), nf)])
            hid[:, pl.ds(pl.multiple_of(j * nf, nf), nf)] = (g * jax.nn.sigmoid(g) * u).astype(bf16)
            return 0
        lax.fori_loop(0, ff // nf, inner, 0)

        def outer(j, _):
            cols = pl.ds(pl.multiple_of(j * nd, nd), nd)
            out = dg(hid[...], down[:, cols]) * weight
            y[half(zz), :, :, r * part:(r + 1) * part, cols] = out.astype(bf16).reshape(4, 2, part, nd)
            return 0
        lax.fori_loop(0, width // nd, outer, 0)
        sums.go(zz * 4 + r, lambda: (y.at[half(zz), :, 1 - place.c, rows_of(r)],
                                     kin.at[half(zz), :, rows_of(r)], twin()))

    def own(zz, dx, r):
        return y.at[half(zz), (place.x + dx) % 4, place.c, rows_of(r)]

    def got(zz, dx, r):
        return kin.at[half(zz), (place.x + dx) % 4, rows_of(r)]

    def onward(r):
        return (plus, minus, 1, bp) if r % 2 == 0 else (minus, plus, 3, bm)

    def direct(r):
        return (minus, 3, bm) if r % 2 == 0 else (plus, 1, bp)

    def chip_sums(zz, r):
        sums.arrive(zz * 4 + r, kin.at[half(zz), :, rows_of(r)], twin())
        to, dx, into = direct(r)
        add_rows(own(zz, 2, r), [own(zz, 2, r), got(zz, 2, r)], part)
        sums.go(8 + zz * 4 + r, lambda: (own(zz, 2, r), ap.at[zz, r], onward(r)[0]()))
        add_rows(own(zz, dx, r), [own(zz, dx, r), got(zz, dx, r)], part)
        sums.go(16 + zz * 4 + r, lambda: (own(zz, dx, r), into.at[zz, rows_of(r)], to()))

    def relay(zz, r):
        to, back, dx, into = onward(r)
        sums.arrive(8 + zz * 4 + r, ap.at[zz, r], back())
        add_rows(own(zz, dx, r), [own(zz, dx, r), got(zz, dx, r), ap.at[zz, r]], part)
        sums.go(24 + zz * 4 + r, lambda: (own(zz, dx, r), into.at[zz, rows_of(r)], to()))

    def settled(zz, r):
        sums.arrive(16 + zz * 4 + r, direct(r)[2].at[zz, rows_of(r)], plus())
        sums.arrive(24 + zz * 4 + r, onward(r)[3].at[zz, rows_of(r)], plus())
        return [own(zz, 0, r), got(zz, 0, r), bp.at[zz, rows_of(r)], bm.at[zz, rows_of(r)]]

    def cross(r):
        sources = settled(1, r)
        add_rows(own(1, 0, r), sources, part)
        sums.go(32 + r, lambda: (own(1, 0, r), zb.at[rows_of(r)], over()))

    def last(r):
        sources = settled(0, r)
        sums.arrive(32 + r, zb.at[rows_of(r)], over())
        add_rows(out_ref.at[rows_of(r)], [mid.at[rows_of(r)]] + sources + [zb.at[rows_of(r)]], part)

    for k in range(len(ORDER) + 4):
        if k < len(ORDER):
            gather.advance(k)
        for lag, stage in ((1, compute), (2, chip_sums), (3, relay)):
            if 0 <= k - lag < len(ORDER):
                stage(*ORDER[k - lag])
        if k >= 4 and ORDER[k - 4][0] == 1:
            cross(ORDER[k - 4][1])
    for r in range(PIECES):
        last(r)

    def head_out(c, _):
        @pl.when(c != place.e)
        def _():
            head_copy(c).wait_send()
        return 0
    lax.fori_loop(0, chunks, head_out, 0)
    weights_in.finish()
    columns_in.finish()
    routed.finish()
    sums.finish()


def layer_call(tokens, docs, ids, gains, packed, columns, conv, rate, hgain, router, expert_in, expert_out):
    tok, width = tokens.shape
    rows, cols = packed.shape
    ff = expert_out.shape[0]
    seq = 16 * tok
    V, A = pl.BlockSpec(memory_space=pltpu.VMEM), pl.BlockSpec(memory_space=pl.ANY)
    S = pl.BlockSpec(memory_space=pltpu.SMEM)

    def vm(*s):
        return pltpu.VMEM(s, bf16)

    def vf(*s):
        return pltpu.VMEM(s, f32)
    sem = pltpu.SemaphoreType.DMA
    return pl.pallas_call(
        layer_kernel,
        out_shape=jax.ShapeDtypeStruct((tok, width), bf16),
        in_specs=[V, V, V, V, V, V, V, S, V, V, A, A],
        out_specs=V,
        scratch_shapes=[
            vm(2, 4, 2, tok, width + HD), vm(16, rows, cols), vm(16, width), vm(16, HD, HD), vf(seq + 8, 3 * HD),
            vm(seq, HD), vf(seq, 16), vf(seq + 8, HD), vf(seq // C, 2 * C, HD), vf(seq // C, 2 * C, HD),
            vm(seq // C, C, HD), vm(tok, 16 * HD), vf(tok, width), vm(2, 4, 2, tok, width), vm(2, 4, tok, width),
            vm(2, PIECES, tok // PIECES, width), vm(2, tok, width), vm(2, tok, width), vm(tok, width),
            vm(width, 2 * ff), vm(ff, width), vm(8 * tok // PIECES, ff),
            sem((SEM_ALL,)), sem((SEM_ALL,)), sem((2,))],
        compiler_params=pltpu.CompilerParams(collective_id=0, has_side_effects=True,
                                             vmem_limit_bytes=60 * 1024 * 1024),
        name="whole_layer",
    )(tokens, docs, ids, gains, packed, columns, conv, rate, hgain, router, expert_in, expert_out)


def on_device(tokens, doc_ids, route_ids, norm_gain, proj_weight, gating_weight, block_scale,
              conv_weight, decay_rate, head_gain, out_weight, moe_gain, router_weight,
              expert_in, expert_out):
    scale = jnp.repeat(block_scale[0, 0].astype(f32), HD)
    scaled = (proj_weight[:, 0, :].astype(f32) * scale[None, :]).astype(bf16)
    gating = jnp.pad(gating_weight[:, :, 0].T, ((0, 14), (0, 3 * HD)))
    packed = jnp.concatenate([scaled, gating], 0)
    return layer_call(
        tokens[0], doc_ids, route_ids[0], jnp.stack([norm_gain, moe_gain]), packed, out_weight[0],
        conv_weight[0], decay_rate, head_gain.reshape(1, -1), router_weight, expert_in[0], expert_out[0])[None]


def solution(mesh):
    placed = (
        P("fsdp", "expert", None),
        P("fsdp", None),
        P("fsdp", "expert", None),
        P(),
        P("fsdp", "expert", None),
        P("fsdp", None, "expert"),
        P("fsdp", "expert", None),
        P("expert", None, None),
        P("expert"),
        P(),
        P("expert", None, "fsdp"),
        P(),
        P(),
        P("expert", None, None),
        P("expert", None, None),
    )
    return jax.shard_map(
        on_device, mesh=mesh, in_specs=placed, out_specs=P("fsdp", "expert", None), check_vma=False
    )
```

time: 279 us -> 328 us (1.18)
  the two profiles are of different devices: /device:TPU:39 before, /device:TPU:124 now
where the time goes in v4:
time: 328 us; the launch traced here: 327 us
  Pallas kernels  317 us (97%)
  local copies, waits for them, and re-layouts  6.59 us (2%)
  other arithmetic  3.54 us (1%)
    pallas_call x1, Pallas kernels, layer_call(): pl.pallas_call(layer_kernel, out_shape=jax.ShapeDtypeStruct((tok, width),...  317 us

profile of v4, /device:TPU:124, one launch (start us, length us, event | category | flops | bytes accessed | tf_op | source)
XLA Modules:
  0.0 327.3 jit_solution(15685784688779970969)
XLA Ops:
  0.7 0.7 bitcast_convert_fusion
  1.3 0.1 broadcast_bitcast_fusion
  1.4 0.7 stack.9
  2.1 0.7 stack.10
  2.8 0.6 pad_maximum_fusion.gains_ref
  3.4 1.4 copy.16
  4.8 0.9 fusion.1
  5.7 1.3 fusion.2.pack_ref
  7.1 1.8 copy.17.router_ref
  8.9 316.5 %whole_layer.1 = bf16[128,2048]{1,0:T(8,128)(2,1)} custom-call(bf16[128,2048]{1,0:T(8,128)(2,1)} %bitcast.22, s32[1,2048]{1,0:T(1,128)} %docs_ref.1, s32[128,10]{1,0:T(8,128)} %bitcast.23, bf16[2,2048]{1,0:T(2,128)(2,1)} %pad_maximum_fusion.gains_ref, bf16[144,512]{1,0:T(8,128)(2,1)} %fusion.2.pack_ref, bf16[128,128]{1,0:T(8,128)(2,1)} %bitcast.24, ...), custom_call_target="tpu_custom_call" | custom-call | tf_op jit(solution)/shard_map/whole_layer/pallas_call | solution.py:573
  325.5 1.9 copy.20

commit v5 on v3

--- a/solution.py
+++ b/solution.py
@@ -65,23 +65,23 @@
     h1 = r1.astype(bf16)
     h2 = (r1 - h1.astype(f32)).astype(bf16)
     cum = dg(tri, h0) + (dg(tri, h1) + dg(tri, h2))
-    doc_row = docs_ref[pl.ds(c, 1), :]
+    doc_row = docs_ref[0:1, pl.ds(r0, C)].astype(f32)
     keep = jnp.logical_and(low, doc_col == doc_row)
     gap = cum - cum.T
     decay = jnp.where(keep, jnp.exp(jnp.where(keep, gap, 0.0)), 0.0)
     start = jnp.where(doc_col == docw[7:8, :], jnp.exp(cum), 0.0)
-    kk = mm(k, k, NT)
-    qk = mm(q, k, NT) * decay
+    kk = mm(k, k, NT, passes=1)
+    qk = mm(q, k, NT, passes=1) * decay
     L = jnp.where(row > col, beta * kk * decay, 0.0)
     eye = (row == col).astype(f32)
     T = eye - jnp.where((row >> 1) == (col >> 1), L, 0.0)
     for sh in range(1, 7):
         m = jnp.logical_and((row >> (sh + 1)) == (col >> (sh + 1)), (row >> sh) != (col >> sh))
-        T = T - mm(T, mm(jnp.where(m, L, 0.0), T))
-    UW = mm(T, jnp.concatenate([beta * v, beta * start * k], axis=1))
+        T = T - mm(T, mm(jnp.where(m, L, 0.0), T, passes=1), passes=1)
+    UW = mm(T, jnp.concatenate([beta * v, beta * start * k], axis=1), passes=1)
     kend = k * decay.T[:, C - 1:C]
-    PUW = mm(qk, UW)
-    KUW = mm(kend, UW, TN)
+    PUW = mm(qk, UW, passes=1)
+    KUW = mm(kend, UW, TN, passes=1)
     M = eye * start[C - 1:C, :] - KUW[:, HD:]
     Qp = start * q - PUW[:, HD:]
     return Qp, M, PUW[:, :HD], KUW[:, :HD]
@@ -163,9 +163,11 @@
     def minus(self, zz, h):
         self.go(6 + zz * 2 + h, zz, 0, h, (0, 3))
 
-    def begin(self):
+    def begin(self, paced=True):
+        self.paced = paced
         for h in range(2):
-            self.go(h, 0, 0, h, (1, 0))
+            if h == 0 or not paced:
+                self.go(h, 0, 0, h, (1, 0))
             self.plus(0, h)
             self.minus(0, 1 - h)
         self.swap(0, 0, 0)
@@ -180,7 +182,10 @@
         self.take(6 + zz * 2, zz, 1, 0)
 
     def from_z(self, h):
-        self.take(h, 1, 0, h)
+        self.copies.arrive(h, self.ref(1, 0, h), self.peer(0, 1))
+        if h == 0 and self.paced:
+            self.go(1, 0, 0, 1, (1, 0))
+        self.swap(1, 0, h)
         self.plus(1, h)
         self.minus(1, h)
 
@@ -207,7 +212,7 @@
 SEM_ALL = SEM_SUMS + 22
 
 
-def layer_kernel(tok_ref, docs_ref, ids_ref, gain_ref, pack_ref, conv_ref, rate_ref, hgain_ref, mgain_ref,
+def layer_kernel(tok_ref, docs_ref, ids_ref, gains_ref, pack_ref, conv_ref, rate_ref, hgain_ref,
                  router_ref, ein_ref, eout_ref, out_ref,
                  full, w, win, branch, gate_ref, docc, maps, adds, obuf, heads, mid, y, kin, ap, am, bp, bm, zb,
                  up, down, hid, send, recv, load):
@@ -232,7 +237,7 @@
     for copy in loads:
         copy.start()
     w[fsdp] = pack_ref[...]
-    full[place.e, :, :width] = rms_scale(tok_ref[...].astype(f32), gain_ref[...]).astype(bf16)
+    full[place.e, :, :width] = rms_scale(tok_ref[...].astype(f32), gains_ref[0:1, :]).astype(bf16)
     pl.semaphore_wait(barrier, len(peers))
 
     tokens = Copies(send, recv, SEM_TOKENS)
@@ -276,7 +281,8 @@
 
     def spread(c, _):
         at = pl.ds(pl.multiple_of(c * C + 8, 8), C)
-        docc[at, :] = jnp.broadcast_to(docs_ref[pl.ds(c, 1), :], (C, C)).T
+        docs = docs_ref[0:1, pl.ds(pl.multiple_of(c * C, C), C)].astype(f32)
+        docc[at, :] = jnp.broadcast_to(docs, (C, C)).T
         return 0
     lax.fori_loop(0, chunks, spread, 0)
     for d in range(1, 4):
@@ -320,7 +326,7 @@
 
     def other_half():
         project(1)
-        spreads.begin()
+        spreads.begin(paced=False)
 
     events = {
         1: lambda: gather.from_x(1),
@@ -390,7 +396,7 @@
         mid[:, cols] = tok_ref[:, cols].astype(f32) + dg(heads[...], y[:, :, cols].reshape(16 * HD, nd))
         return 0
     lax.fori_loop(0, width // nd, out_project, 0)
-    moe_in = rms_scale(mid[...], mgain_ref[...]).astype(bf16)
+    moe_in = rms_scale(mid[...], gains_ref[1:2, :]).astype(bf16)
     full[place.e, :, :width] = moe_in
     logits = dg(full[place.e, :, :width], router_ref[...])
     lane = lax.broadcasted_iota(jnp.int32, (tok, HD), 1)
@@ -524,7 +530,7 @@
     sums.finish()
 
 
-def layer_call(tokens, docs, ids, gain, packed, conv, rate, hgain, mgain, router, expert_in, expert_out):
+def layer_call(tokens, docs, ids, gains, packed, conv, rate, hgain, router, expert_in, expert_out):
     tok, width = tokens.shape
     rows, cols = packed.shape
     ff = expert_out.shape[0]
@@ -541,7 +547,7 @@
     return pl.pallas_call(
         layer_kernel,
         out_shape=jax.ShapeDtypeStruct((tok, width), bf16),
-        in_specs=[V, V, V, V, V, V, S, V, V, V, A, A],
+        in_specs=[V, V, V, V, V, V, S, V, V, A, A],
         out_specs=V,
         scratch_shapes=[
             vm(16, tok, width + HD), vm(16, rows, cols), vf(seq + 8, 3 * HD), vm(seq, HD), vf(seq, HD),
@@ -552,7 +558,7 @@
         compiler_params=pltpu.CompilerParams(collective_id=0, has_side_effects=True,
                                              vmem_limit_bytes=60 * 1024 * 1024),
         name="whole_layer",
-    )(tokens, docs, ids, gain, packed, conv, rate, hgain, mgain, router, expert_in, expert_out)
+    )(tokens, docs, ids, gains, packed, conv, rate, hgain, router, expert_in, expert_out)
 
 
 def on_device(tokens, doc_ids, route_ids, norm_gain, proj_weight, gating_weight, block_scale,
@@ -564,8 +570,8 @@
         [scaled, jnp.pad(gating_weight[:, :, 0], ((0, 0), (0, HD - 2))), out_weight[0]], 1)
     router = jnp.pad(jnp.concatenate([router_weight, router_weight], 1), ((0, 0), (0, HD - 2 * EXPERTS)))
     return layer_call(
-        tokens[0], doc_ids[0].astype(f32).reshape(-1, C), route_ids[0], norm_gain.reshape(1, -1), packed,
-        conv_weight[0], decay_rate, head_gain.reshape(1, -1), moe_gain.reshape(1, -1), router,
+        tokens[0], doc_ids, route_ids[0], jnp.stack([norm_gain, moe_gain]), packed,
+        conv_weight[0], decay_rate, head_gain.reshape(1, -1), router,
         expert_in[0], expert_out[0])[None]
 
 

time: 279 us -> 265 us (0.950)
  the two profiles are of different devices: /device:TPU:39 before, /device:TPU:224 now
where the time goes in v5:
time: 265 us
  Pallas kernels  253 us (95%)
  local copies, waits for them, and re-layouts  6.71 us (3%)
  other arithmetic  4.57 us (2%)
    pallas_call x1, Pallas kernels, layer_call(): pl.pallas_call(layer_kernel, out_shape=jax.ShapeDtypeStruct((tok, width),...  253 us

profile of v5, /device:TPU:224, one launch (start us, length us, event | category | flops | bytes accessed | tf_op | source)
XLA Modules:
  0.0 264.6 jit_solution(16334566423990893924)
XLA Ops:
  0.7 0.7 bitcast_convert_fusion
  1.3 0.1 broadcast_bitcast_fusion
  1.4 0.7 stack.9
  2.1 0.7 stack.10
  2.8 0.6 pad_maximum_fusion.1.gains_ref
  3.4 0.8 copy.21
  4.2 1.4 copy.20
  5.6 0.9 fusion.2
  6.5 1.5 fusion.4.pack_ref
  8.0 0.9 pad_maximum_fusion
  8.9 0.3 copy.22
  9.2 0.9 pad.9.router_ref
  10.1 252.7 %whole_layer.1 = bf16[128,2048]{1,0:T(8,128)(2,1)} custom-call(bf16[128,2048]{1,0:T(8,128)(2,1)} %bitcast.20, s32[1,2048]{1,0:T(1,128)} %docs_ref.1, s32[128,10]{1,0:T(8,128)} %bitcast.21, bf16[2,2048]{1,0:T(2,128)(2,1)} %pad_maximum_fusion.1.gains_ref, bf16[128,768]{1,0:T(8,128)(2,1)} %fusion.4.pack_ref, bf16[4,384]{1,0:T(4,128)(2,1)} %bitcast.24, ...), custom_call_target="tpu_custom_call" | custom-call | tf_op jit(solution)/shard_map/whole_layer/pallas_call | solution.py:547
  262.7 1.9 copy.25

commit v6 on v5

--- a/solution.py
+++ b/solution.py
@@ -489,15 +489,13 @@
     gather.from_far(0)
     compute(0, 2)
     gather.from_x(1)
+    compute(1, 0)
+    gather.from_far(1)
     far(0)
-    compute(1, 0)
-    near(0)
-    gather.from_far(1)
     compute(1, 3)
-    relay(0)
-    compute(1, 1)
     compute(1, 2)
     far(1)
+    compute(1, 1)
     near(1)
     relay(1)
     chip_sum(1, 0)
@@ -505,6 +503,8 @@
         settle(1, h)
         add_rows(own(1, 0), [bp.at[1], bm.at[1]], h * half, half)
         sums.go(20 + h, lambda part=part: (own(1, 0).at[part], zb.at[part], over()))
+    near(0)
+    relay(0)
     chip_sum(0, 0)
     for h, part in ((0, low), (1, high)):
         settle(0, h)

time: 265 us -> 259 us (0.977)
  Pallas kernels: 253 us -> 247 us
    pallas_call x1, Pallas kernels: 253 us -> 247 us  [layer_call(): pl.pallas_call(layer_kernel, out_shape=jax.ShapeDtypeStruct((tok, width),...]
where the time goes in v6:
time: 259 us
  Pallas kernels  247 us (95%)
  local copies, waits for them, and re-layouts  6.71 us (3%)
  other arithmetic  4.57 us (2%)
    pallas_call x1, Pallas kernels, layer_call(): pl.pallas_call(layer_kernel, out_shape=jax.ShapeDtypeStruct((tok, width),...  247 us

profile of v6, /device:TPU:224, one launch (start us, length us, event | category | flops | bytes accessed | tf_op | source)
XLA Modules:
  0.0 258.8 jit_solution(8490838206718915312)
XLA Ops:
  0.7 0.7 bitcast_convert_fusion
  1.3 0.1 broadcast_bitcast_fusion
  1.4 0.7 stack.9
  2.1 0.7 stack.10
  2.8 0.6 pad_maximum_fusion.1.gains_ref
  3.4 0.8 copy.21
  4.2 1.4 copy.20
  5.6 0.9 fusion.2
  6.5 1.5 fusion.4.pack_ref
  8.0 0.9 pad_maximum_fusion
  8.9 0.3 copy.22
  9.2 0.9 pad.9.router_ref
  10.1 246.8 %whole_layer.1 = bf16[128,2048]{1,0:T(8,128)(2,1)} custom-call(bf16[128,2048]{1,0:T(8,128)(2,1)} %bitcast.20, s32[1,2048]{1,0:T(1,128)} %docs_ref.1, s32[128,10]{1,0:T(8,128)} %bitcast.21, bf16[2,2048]{1,0:T(2,128)(2,1)} %pad_maximum_fusion.1.gains_ref, bf16[128,768]{1,0:T(8,128)(2,1)} %fusion.4.pack_ref, bf16[4,384]{1,0:T(4,128)(2,1)} %bitcast.24, ...), custom_call_target="tpu_custom_call" | custom-call | tf_op jit(solution)/shard_map/whole_layer/pallas_call | solution.py:547
  256.9 1.9 copy.25

commit v7 on v6

--- a/solution.py
+++ b/solution.py
@@ -324,14 +324,14 @@
     outs = Copies(send, recv, SEM_OUT)
     spreads = Gather(y, outs, place, width)
 
-    def other_half():
-        project(1)
+    def half_here():
+        gather.from_far(1)
         spreads.begin(paced=False)
 
     events = {
         1: lambda: gather.from_x(1),
-        2: lambda: gather.from_far(1),
-        3: other_half,
+        2: half_here,
+        3: lambda: project(1),
         4: lambda: spreads.from_x(0),
         5: lambda: spreads.from_far(0),
         6: lambda: spreads.from_z(0),
@@ -351,7 +351,6 @@
         return 0
     lax.fori_loop(0, chunks // 2, two_chunks, 0)
     tokens.finish()
-    spreads.from_x(1)
 
     def head_copy(c):
         return pltpu.make_async_remote_copy(
@@ -373,8 +372,9 @@
             head_copy(c).start()
         return two[C:, :]
     S = lax.fori_loop(0, chunks // 2, advance, jnp.zeros((HD, HD), f32))
+    spreads.from_x(1)
+    lax.fori_loop(chunks // 2, chunks, advance, S)
     spreads.from_far(1)
-    lax.fori_loop(chunks // 2, chunks, advance, S)
     for zz in range(2):
         for dx in range(4):
             spreads.swapped(zz, dx)

time: 259 us -> 246 us (0.950); the launches traced: 259 us -> 242 us
  Pallas kernels: 247 us -> 230 us
    pallas_call x1, Pallas kernels: 247 us -> 230 us  [layer_call(): pl.pallas_call(layer_kernel, out_shape=jax.ShapeDtypeStruct((tok, width),...]
where the time goes in v7:
time: 246 us; the launch traced here: 242 us
  Pallas kernels  230 us (93%)
  local copies, waits for them, and re-layouts  6.71 us (3%)
  other arithmetic  4.57 us (2%)
    pallas_call x1, Pallas kernels, layer_call(): pl.pallas_call(layer_kernel, out_shape=jax.ShapeDtypeStruct((tok, width),...  230 us

profile of v7, /device:TPU:224, one launch (start us, length us, event | category | flops | bytes accessed | tf_op | source)
XLA Modules:
  0.0 241.6 jit_solution(9979246276745988451)
XLA Ops:
  0.7 0.7 bitcast_convert_fusion
  1.3 0.1 broadcast_bitcast_fusion
  1.4 0.7 stack.9
  2.1 0.7 stack.10
  2.8 0.6 pad_maximum_fusion.1.gains_ref
  3.4 0.8 copy.21
  4.2 1.4 copy.20
  5.6 0.9 fusion.2
  6.5 1.5 fusion.4.pack_ref
  8.0 0.9 pad_maximum_fusion
  8.9 0.3 copy.22
  9.2 0.9 pad.9.router_ref
  10.1 229.7 %whole_layer.1 = bf16[128,2048]{1,0:T(8,128)(2,1)} custom-call(bf16[128,2048]{1,0:T(8,128)(2,1)} %bitcast.20, s32[1,2048]{1,0:T(1,128)} %docs_ref.1, s32[128,10]{1,0:T(8,128)} %bitcast.21, bf16[2,2048]{1,0:T(2,128)(2,1)} %pad_maximum_fusion.1.gains_ref, bf16[128,768]{1,0:T(8,128)(2,1)} %fusion.4.pack_ref, bf16[4,384]{1,0:T(4,128)(2,1)} %bitcast.24, ...), custom_call_target="tpu_custom_call" | custom-call | tf_op jit(solution)/shard_map/whole_layer/pallas_call | solution.py:547
  239.8 1.9 copy.25

commit v8 on v7

--- a/solution.py
+++ b/solution.py
@@ -324,13 +324,13 @@
     outs = Copies(send, recv, SEM_OUT)
     spreads = Gather(y, outs, place, width)
 
-    def half_here():
-        gather.from_far(1)
+    def half_near():
+        gather.from_x(1)
         spreads.begin(paced=False)
 
     events = {
-        1: lambda: gather.from_x(1),
-        2: half_here,
+        1: half_near,
+        2: lambda: gather.from_far(1),
         3: lambda: project(1),
         4: lambda: spreads.from_x(0),
         5: lambda: spreads.from_far(0),

time: 246 us -> 246 us (level)
  no operation moved by 1% of the time
where the time goes in v8:
time: 246 us; the launch traced here: 244 us
  Pallas kernels  232 us (94%)
  local copies, waits for them, and re-layouts  6.71 us (3%)
  other arithmetic  4.57 us (2%)
    pallas_call x1, Pallas kernels, layer_call(): pl.pallas_call(layer_kernel, out_shape=jax.ShapeDtypeStruct((tok, width),...  232 us

profile of v8, /device:TPU:224, one launch (start us, length us, event | category | flops | bytes accessed | tf_op | source)
XLA Modules:
  0.0 244.0 jit_solution(9048633426720366818)
XLA Ops:
  0.7 0.7 bitcast_convert_fusion
  1.3 0.1 broadcast_bitcast_fusion
  1.4 0.7 stack.9
  2.1 0.7 stack.10
  2.8 0.6 pad_maximum_fusion.1.gains_ref
  3.4 0.8 copy.21
  4.2 1.4 copy.20
  5.6 0.9 fusion.2
  6.5 1.5 fusion.4.pack_ref
  8.0 0.9 pad_maximum_fusion
  8.9 0.3 copy.22
  9.2 0.9 pad.9.router_ref
  10.1 232.1 %whole_layer.1 = bf16[128,2048]{1,0:T(8,128)(2,1)} custom-call(bf16[128,2048]{1,0:T(8,128)(2,1)} %bitcast.20, s32[1,2048]{1,0:T(1,128)} %docs_ref.1, s32[128,10]{1,0:T(8,128)} %bitcast.21, bf16[2,2048]{1,0:T(2,128)(2,1)} %pad_maximum_fusion.1.gains_ref, bf16[128,768]{1,0:T(8,128)(2,1)} %fusion.4.pack_ref, bf16[4,384]{1,0:T(4,128)(2,1)} %bitcast.24, ...), custom_call_target="tpu_custom_call" | custom-call | tf_op jit(solution)/shard_map/whole_layer/pallas_call | solution.py:547
  242.1 1.9 copy.25
